TPU v7x, 128 devices: a whole 4x4x4 slice. The times are simulated.
128 devices in a mesh: grp: 4 (over z), shard: 32 (over y, x, core).
Axes of the slice: x: 4, y: 4, z: 4, core: 2. Of those that a mesh axis runs over, the one named last changes fastest.
Arguments:
- context: bfloat16 [196608, 2048], P(('grp', 'shard')), may hold values from -24 to 24
- out_grad: bfloat16 [196608, 4096], P(('grp', 'shard')), may hold values from -0.013671875 to 0.013671875
- old_master: float32 [32, 4, 131072], P('shard', 'grp'), may hold values from -0.125 to 0.125
- old_mom1: float32 [32, 4, 131072], P('shard', 'grp'), may hold values from -6 to 6
- old_mom2: float32 [32, 4, 131072], P('shard', 'grp'), may hold values from 0.05 to 1
- old_lengths: int32 [32, 4], P('shard'), may hold values from 1 to 131072, 262144 in all within a row
Outputs:
- new_master: float32 [32, 64, 4096], P('shard', 'grp')
- new_mom1: float32 [32, 64, 4096], P('shard', 'grp')
- new_mom2: float32 [32, 64, 4096], P('shard', 'grp')
- weights_bf16: bfloat16 [32, 64, 4096], P('shard')
Inputs may be any that keep to these rules, and one draw needn't show every extreme that they name: `old_lengths`: each row sums to 262144, and its largest entry is exactly 131072.
All inputs are finite; a program needn't handle non-finite values.
Results may differ from a plain program's by a relative error of at most 0.0055.
Values may be sent and summed in bfloat16 or wider, within the bound.
No kernel may reach another device: no remote copies, remote signals or barrier semaphores. Data moves between devices by JAX's collectives and lax.ppermute only.
A program may use at most 256 MiB of HBM per device.

v0:
```python
import jax
import jax.numpy as jnp
from jax import lax
from jax.sharding import PartitionSpec as P

beta_one = 0.9
beta_two = 0.95
step_size = 0.01
epsilon = 1e-08


def contract(columns, out_grad):
    return lax.dot_general(
        columns, out_grad, (((0,), (0,)), ((), ())), preferred_element_type=jnp.float32
    )


def local(context, out_grad, old_master, old_mom1, old_mom2, old_lengths):
    groups = lax.axis_size("grp")
    shards = lax.axis_size("shard")
    my_group = lax.axis_index("grp")
    tok_rows, head_width = context.shape
    model_width = out_grad.shape[1]
    rows_own = head_width // (shards * groups)
    block = rows_own * model_width
    slice_total = groups * block
    lengths = old_lengths[0]
    piece_starts = jnp.cumsum(lengths) - lengths
    stacked = jnp.concatenate([old_master[0], old_mom1[0], old_mom2[0]], axis=0)
    column = jnp.arange(block, dtype=jnp.int32)[None, :]
    gathered = lax.all_gather(stacked[None], "grp", axis=0, tiled=True)
    padded = jnp.pad(gathered, ((0, 0), (0, 0), (slice_total, slice_total)))
    own_start = my_group * block
    state = jnp.zeros((3, block), jnp.float32)
    for source in range(groups):
        begin = piece_starts[source]
        window = lax.dynamic_slice(padded[source], (0, own_start - begin + slice_total), (3, block))
        inside = (own_start + column >= begin) & (own_start + column < begin + lengths[source])
        state = state + jnp.where(inside, window, 0.0)
    state = state.reshape(3, rows_own, model_width)
    ordered = (
        context.reshape(tok_rows, shards, groups, rows_own)
        .transpose(0, 2, 1, 3)
        .reshape(tok_rows, head_width)
    )
    gradient = lax.psum_scatter(
        contract(ordered, out_grad), ("grp", "shard"), scatter_dimension=0, tiled=True
    )
    first_new = beta_one * state[1] + (1.0 - beta_one) * gradient
    second_new = beta_two * state[2] + (1.0 - beta_two) * gradient * gradient
    master_new = state[0] - step_size * first_new / (jnp.sqrt(second_new) + epsilon)
    weights = lax.all_gather(master_new.astype(jnp.bfloat16)[None], "grp", axis=1, tiled=True)
    return (master_new[None], first_new[None], second_new[None], weights)


def solution(mesh):
    placed = (
        P(("grp", "shard"), None),
        P(("grp", "shard"), None),
        P("shard", "grp", None),
        P("shard", "grp", None),
        P("shard", "grp", None),
        P("shard", None),
    )
    return jax.shard_map(
        local,
        mesh=mesh,
        in_specs=placed,
        out_specs=(
            P("shard", "grp", None),
            P("shard", "grp", None),
            P("shard", "grp", None),
            P("shard", None, None),
        ),
        check_vma=False,
    )
```

profile of v0, /device:TPU:0, one launch (start us, length us, event | category | flops | bytes accessed | tf_op | source)
XLA Modules:
  0.0 776.8 jit_solution(14124925788595460716)
XLA Ops:
  8.0 0.0 all-gather.5.cloned.1.call-start
  8.0 4.1 maximum_bitcast_fusion
  12.2 0.0 reduce-scatter.2.cloned.1.call-start
  12.2 8.7 %copy.12 = bf16[1536,2048]{0,1:T(8,128)(2,1)} copy(bf16[1536,2048]{1,0:T(8,128)(2,1)} %param.6) | data formatting | bytes 12582912 | tf_op args[0]
  20.9 3.4 copy.13
  24.4 32.4 %fusion.23 = f32[2048,4096]{1,0:T(8,128)} fusion(bf16[1536,2048]{0,1:T(8,128)(2,1)S(1)} %bitcast.51, bf16[1536,4096]{1,0:T(8,128)(2,1)} %param.7), kind=kOutput, calls=%fused_computation.40 | convolution fusion | flops 25769803776 | bytes 52428800 | tf_op jit(solution)/shard_map/dot_general | solution.py:13
  56.8 0.0 reduce-scatter.2.cloned.1.call-update
  56.8 0.6 copy-done
  57.5 0.2 reduce-window.9
  57.6 0.6 fusion.22
  60.8 0.7 fusion.21
  66.6 1.4 fusion.16
  68.0 1.4 fusion.14
  69.4 37.2 %all-gather.5.cloned.1.call-done = f32[4,3,131072]{2,1,0:T(4,128)} async-done(((f32[1,3,131072]{2,1,0:T(4,128)}), f32[4,3,131072]{2,1,0:T(4,128)}) %all-gather.5.cloned.1.call-update) | async-done | bytes 6291472 | tf_op jit(solution)/shard_map/all_gather | solution.py:31
  106.6 20.8 %pad_slice_fusion.3 = (f32[1,3,655360]{2,1,0:T(4,128)S(1)}, f32[1,3,655360]{2,1,0:T(4,128)}, f32[1,3,655360]{2,1,0:T(4,128)}, f32[1,3,655360]{2,1,0:T(4,128)}) fusion(f32[4,3,131072]{2,1,0:T(4,128)} %all-gather.5.cloned.1.call-done), kind=kLoop, calls=%fused_computation.3 | loop fusion | bytes 37748736 | tf_op jit(solution)/shard_map/slice | solution.py:37
  127.4 4.1 fusion
  131.5 2.2 fusion.4
  133.7 0.1 squeeze.57
  133.7 0.1 mul.52
  133.8 0.1 mul.45
  133.9 620.0 %reduce-scatter.2.cloned.1.call-done = f32[16,4096]{1,0:T(8,128)} async-done(((f32[2048,4096]{1,0:T(8,128)}), f32[16,4096]{1,0:T(8,128)}) %reduce-scatter.2.cloned.1.call-update) | async-done | bytes 262160 | tf_op jit(solution)/shard_map/reduce_scatter | solution.py:46
  753.9 1.9 fusion.20
  755.7 12.8 %all-gather.1 = bf16[64,4096]{1,0:T(8,128)(2,1)S(1)} all-gather(bf16[16,4096]{1,0:T(8,128)(2,1)S(1)} %get-tuple-element.7), channel_id=3, replica_groups=mesh['grp'=4,'shard'=32] {'grp'}, dimensions={0}, use_global_device_ids=true | all-gather | bytes 655360 | tf_op jit(solution)/shard_map/all_gather | solution.py:52
  768.5 0.8 copy.15
  (3 shorter events, 0.0 us)
Async XLA Ops:
  8.0 98.6 %all-gather.5.cloned.1.call-start = ((), (), s32[]{:S(2)}) async-start(), calls=%async_computation.2 | async-start | bytes 10485760 | tf_op jit(solution)/shard_map/all_gather | solution.py:31
  12.2 741.7 %reduce-scatter.2.cloned.1.call-start = ((), (), s32[]{:S(2)}) async-start(), calls=%async_computation.1 | async-start | bytes 33816576 | tf_op jit(solution)/shard_map/reduce_scatter | solution.py:46
  56.8 0.7 copy-start
Sparse Core Ops, SparseCore 0:
  12.3 94.2 all-gather.4
Sparse Core Ops, SparseCore 1:
  56.9 696.9 reduce-scatter.1
where the time goes:
time: 777 us
  waiting for transfers between devices  657 us (85%)
  local copies, waits for them, and re-layouts  35.7 us (5%)
  matrix products  32.4 us (4%)
  between operations  23.2 us (3%)
  other arithmetic  15.3 us (2%)
  blocking collectives  12.8 us (2%)
    reduce_scatter x1, waiting for transfers between devices, local(): lax.psum_scatter(contract(ordered, out_grad), ('grp', 'shard'), scatter_d...  620 us
    all_gather x1, waiting for transfers between devices, local(): gathered = lax.all_gather(stacked[None], 'grp', axis=0, tiled=True)  37.2 us
    dot_general x1, matrix products, contract(): lax.dot_general(columns, out_grad, (((0,), (0,)), ((), ())), preferred_el...  32.4 us
    slice x1, local copies, waits for them, and re-layouts, local(): padded[source]  20.8 us
  transfers between devices with their start and end apart: 2, of which 2 were waited for; matrix products, arithmetic and copies ran while one was open for 10% of the time, Pallas kernels for 0%

commit v1 on v0

v1 whole, which is shorter than its diff:
```python
import jax
import jax.numpy as jnp
from jax import lax
from jax.experimental import pallas as pl
from jax.experimental.pallas import tpu as pltpu
from jax.sharding import PartitionSpec as P

beta_one = 0.9
beta_two = 0.95
step_size = 0.01
epsilon = 1e-08

N_GRP, N_SHARD, SIDE = 4, 32, 4
ROWS = 64
CHUNKS = (2048, 2048)
f32, bf16 = jnp.float32, jnp.bfloat16


def moved(by_core):
    pairs = []
    for z in range(4):
        for y in range(4):
            for x in range(4):
                for c in range(2):
                    axis, shift = by_core[c]
                    to = {"z": z, "y": y, "x": x}
                    to[axis] = (to[axis] + shift) % 4
                    pairs.append(
                        (((z * 4 + y) * 4 + x) * 2 + c, ((to["z"] * 4 + to["y"]) * 4 + to["x"]) * 2 + c)
                    )
    return pairs


FIRST = {k: moved((("x", k), ("y", k))) for k in (1, 2, 3)}
SECOND = {k: moved((("y", k), ("x", k))) for k in (1, 2, 3)}
ALONG_Z = {k: moved((("z", k), ("z", k))) for k in (1, 2, 3)}
SWAP = [(i, i ^ 1) for i in range(128)]


def send(value, pairs):
    return lax.ppermute(value, ("grp", "shard"), pairs)


def row_table():
    shard = lax.axis_index("shard")
    c, x, y = shard % 2, (shard // 2) % 4, shard // 8

    def of(core):
        j = jnp.arange(16, dtype=jnp.int32)
        j1, j2 = j // 4, j % 4
        jx, jy = jnp.where(core == 0, j1, j2), jnp.where(core == 0, j2, j1)
        return 2 * (((y + jy) % 4) * 4 + (x + jx) % 4) + core

    return jnp.concatenate([of(c), of(1 - c)]).astype(jnp.int32)


def call(body, name, steps, in_specs, out_specs, out_shape, moved_bytes, *operands):
    return pl.pallas_call(
        body,
        grid_spec=pltpu.PrefetchScalarGridSpec(
            num_scalar_prefetch=1, grid=(steps,), in_specs=in_specs, out_specs=out_specs
        ),
        out_shape=out_shape,
        name=name,
        cost_estimate=pl.CostEstimate(flops=moved_bytes // 4, bytes_accessed=moved_bytes, transcendentals=0),
        compiler_params=pltpu.CompilerParams(vmem_limit_bytes=40 * 2**20),
    )(*operands)


def for_other_core(table, partial):
    cols = partial.shape[1]

    def body(t, p, o):
        o[0] = p[...].astype(bf16)

    return call(
        body, "for_other_core", 16,
        [pl.BlockSpec((ROWS, cols), lambda i, t: (t[16 + i], 0))],
        pl.BlockSpec((1, ROWS, cols), lambda i, t: (i, 0, 0)),
        jax.ShapeDtypeStruct((16, ROWS, cols), bf16),
        16 * ROWS * cols * 6, table, partial,
    )


def own(cols, place):
    return [
        pl.BlockSpec((ROWS, cols), lambda i, t: (t[place(i)], 0)),
        pl.BlockSpec((1, ROWS, cols), lambda i, t: (place(i), 0, 0)),
    ]


def part(cols, place):
    return pl.BlockSpec((1, ROWS, cols), lambda i, t: (place(i), 0, 0))


def first_sends(table, partial, other):
    cols = partial.shape[1]

    def body(t, p0, r0, p1, r1, plus, minus):
        plus[0] = (p0[...] + r0[0].astype(f32)).astype(bf16)
        minus[0] = (p1[...] + r1[0].astype(f32)).astype(bf16)

    return call(
        body, "first_sends", 4,
        own(cols, lambda i: jnp.where(i < 2, 8 + i, 4 + i)) + own(cols, lambda i: jnp.where(i < 2, 12 + i, 8 + i)),
        [part(cols, lambda i: i)] * 2,
        [jax.ShapeDtypeStruct((4, ROWS, cols), bf16)] * 2,
        8 * ROWS * cols * 8, table, partial, other, partial, other,
    )


def second_sends(table, partial, other, from_minus, from_plus):
    cols = partial.shape[1]

    def body(t, p0, r0, a, p1, r1, b, plus, minus):
        plus[0] = (p0[...] + r0[0].astype(f32) + a[0].astype(f32)).astype(bf16)
        minus[0] = (p1[...] + r1[0].astype(f32) + b[0].astype(f32)).astype(bf16)

    return call(
        body, "second_sends", 2,
        own(cols, lambda i: 4 + i) + [part(cols, lambda i: i)]
        + own(cols, lambda i: 14 + i) + [part(cols, lambda i: 2 + i)],
        [part(cols, lambda i: i)] * 2,
        [jax.ShapeDtypeStruct((2, ROWS, cols), bf16)] * 2,
        4 * ROWS * cols * 10, table, partial, other, from_minus, partial, other, from_plus,
    )


def first_sums(table, partial, other, from_minus, from_plus, far_minus, far_plus):
    cols = partial.shape[1]

    def body(t, p, r, a0, b0, a1, b1, keep, s1, s2, s3):
        i = pl.program_id(0)
        base = p[...] + r[0].astype(f32)

        @pl.when(i == 0)
        def _():
            keep[...] = base + a0[0].astype(f32) + b0[0].astype(f32)

        @pl.when(i == 1)
        def _():
            s1[...] = (base + a0[0].astype(f32) + b0[0].astype(f32)).astype(bf16)

        @pl.when(i == 2)
        def _():
            s2[...] = (base + a1[0].astype(f32) + b1[0].astype(f32)).astype(bf16)

        @pl.when(i == 3)
        def _():
            s3[...] = (base + a1[0].astype(f32) + b1[0].astype(f32)).astype(bf16)

    whole = pl.BlockSpec((ROWS, cols), lambda i, t: (0, 0))
    return call(
        body, "first_sums", 4,
        own(cols, lambda i: i)
        + [
            part(cols, lambda i: jnp.minimum(i, 1)),
            part(cols, lambda i: jnp.minimum(i, 1)),
            part(cols, lambda i: jnp.maximum(i, 2)),
            part(cols, lambda i: jnp.maximum(i - 2, 0)),
        ],
        [whole] * 4,
        [jax.ShapeDtypeStruct((ROWS, cols), f32)] + [jax.ShapeDtypeStruct((ROWS, cols), bf16)] * 3,
        4 * ROWS * cols * 13, table, partial, other, from_plus, far_minus, from_minus, far_plus,
    )


def windows(lengths, pieces):
    groups, my_group = N_GRP, lax.axis_index("grp")
    cap = pieces[0].shape[0] * 128
    block = N_GRP * ROWS * 4096 // N_GRP // N_GRP
    n = block // 128
    starts = jnp.cumsum(lengths) - lengths
    mine = lax.dynamic_index_in_dim(starts, my_group, keepdims=False)
    length = lax.dynamic_index_in_dim(lengths, my_group, keepdims=False)
    target = (my_group + jnp.arange(groups, dtype=jnp.int32)) % groups
    offset = target * block - mine
    row = jnp.clip(offset // 128, -n, cap // 128) + n
    scalars = jnp.concatenate([offset, row, offset % 128, length[None]]).astype(jnp.int32)

    def body(s, piece, keep, s1, s2, s3, held):
        held[pl.ds(n, cap // 128), :] = piece[0]
        lane = lax.broadcasted_iota(jnp.int32, (n, 128), 1)
        at = lax.broadcasted_iota(jnp.int32, (n, 128), 0) * 128 + lane
        for j, out in enumerate((keep, s1, s2, s3)):
            off, first, turn = s[j], s[4 + j], s[8 + j]
            low = held[pl.ds(first, n), :]
            high = held[pl.ds(first + 1, n), :]
            back = lax.rem(128 - turn, 128)
            value = jnp.where(lane < 128 - turn, pltpu.roll(low, back, 1), pltpu.roll(high, back, 1))
            inside = (at + off >= 0) & (at + off < s[12])
            out[0] = jnp.where(inside, value, 0.0).astype(out.dtype)

    spec = pl.BlockSpec((1, n, 128), lambda i, s: (i, 0, 0))
    return pl.pallas_call(
        body,
        grid_spec=pltpu.PrefetchScalarGridSpec(
            num_scalar_prefetch=1,
            grid=(3,),
            in_specs=[pl.BlockSpec((1, cap // 128, 128), lambda i, s: (i, 0, 0))],
            out_specs=[spec] * 4,
            scratch_shapes=[pltpu.VMEM((cap // 128 + 2 * n + 8, 128), f32)],
        ),
        out_shape=[jax.ShapeDtypeStruct((3, n, 128), f32)] + [jax.ShapeDtypeStruct((3, n, 128), bf16)] * 3,
        name="windows",
        cost_estimate=pl.CostEstimate(flops=10**7, bytes_accessed=4 * 10**6, transcendentals=0),
        compiler_params=pltpu.CompilerParams(vmem_limit_bytes=40 * 2**20),
    )(scalars, jnp.stack(pieces))


def local(context, out_grad, old_master, old_mom1, old_mom2, old_lengths):
    width = out_grad.shape[1]
    table = row_table()
    keep, *away = windows(old_lengths[0], [a.reshape(-1, 128) for a in (old_master, old_mom1, old_mom2)])
    arrived = [send(away[k - 1], ALONG_Z[k]) for k in (1, 2, 3)]

    gradient = []
    start = 0
    for cols in CHUNKS:
        partial = lax.dot_general(
            context, out_grad[:, start:start + cols], (((0,), (0,)), ((), ())), preferred_element_type=f32
        )
        start += cols
        other = send(for_other_core(table, partial), SWAP)
        plus, minus = first_sends(table, partial, other)
        from_minus, from_plus = send(plus, FIRST[1]), send(minus, FIRST[3])
        plus, minus = second_sends(table, partial, other, from_minus, from_plus)
        far_minus, far_plus = send(plus, FIRST[1]), send(minus, FIRST[3])
        mine, *away = first_sums(table, partial, other, from_minus, from_plus, far_minus, far_plus)
        for k in (1, 2, 3):
            mine = mine + send(away[k - 1], SECOND[k]).astype(f32)
        rows = lax.all_to_all(mine.reshape(N_GRP, ROWS // N_GRP, cols), "grp", 0, 0, tiled=True)
        gradient.append(jnp.sum(rows, axis=0))
    gradient = jnp.concatenate(gradient, axis=1)

    state = keep
    for value in arrived:
        state = state + value.astype(f32)
    state = state.reshape(3, ROWS // N_GRP, width)
    first_new = beta_one * state[1] + (1.0 - beta_one) * gradient
    second_new = beta_two * state[2] + (1.0 - beta_two) * gradient * gradient
    master_new = state[0] - step_size * first_new / (jnp.sqrt(second_new) + epsilon)
    weights = lax.all_gather(master_new.astype(bf16)[None], "grp", axis=1, tiled=True)
    return (master_new[None], first_new[None], second_new[None], weights)


def solution(mesh):
    placed = (
        P(("grp", "shard"), None),
        P(("grp", "shard"), None),
        P("shard", "grp", None),
        P("shard", "grp", None),
        P("shard", "grp", None),
        P("shard", None),
    )
    return jax.shard_map(
        local,
        mesh=mesh,
        in_specs=placed,
        out_specs=(
            P("shard", "grp", None),
            P("shard", "grp", None),
            P("shard", "grp", None),
            P("shard", None, None),
        ),
        check_vma=False,
    )
```

time: 777 us -> 173 us (0.22)
  waiting for transfers between devices: 657 us -> 21.9 us
  Pallas kernels: 0 us -> 45.3 us
  starting transfers between devices: 0.08 us -> 39.1 us
  local copies, waits for them, and re-layouts: 35.7 us -> 4.35 us
  between operations: 23.2 us -> 0.89 us
  other arithmetic: 15.3 us -> 5.96 us
  matrix products: 32.4 us -> 41.2 us
    reduce_scatter x1 -> x0, waiting for transfers between devices: 620 us -> none  [local(): lax.psum_scatter(contract(ordered, out_grad), ('grp', 'shard'), scatter_d...]
    pallas_call x0 -> x9, Pallas kernels: none -> 45.3 us  [the longest x8 42.5 us: call(): pl.pallas_call(body, grid_spec=pltpu.PrefetchScalarGridSpec(num_scalar_pr...]
    all_gather x1 -> x0, waiting for transfers between devices: 37.2 us -> none  [local(): gathered = lax.all_gather(stacked[None], 'grp', axis=0, tiled=True)]
    ppermute x0 -> x19, starting transfers between devices: none -> 30.7 us  [send(): return lax.ppermute(value, ('grp', 'shard'), pairs)]
    slice x3 -> x0, local copies, waits for them, and re-layouts: 22 us -> none  [the longest x1 20.8 us: local(): padded[source]]
    ppermute x0 -> x19, waiting for transfers between devices: none -> 14.1 us  [send(): return lax.ppermute(value, ('grp', 'shard'), pairs)]
    dot_general x1 -> x2, matrix products: 32.4 us -> 41.2 us  [local(): lax.dot_general(context, out_grad[:, start:start + cols], (((0,), (0,)),...]
    all_to_all x0 -> x2, starting transfers between devices: none -> 8.44 us  [local(): lax.all_to_all(mine.reshape(N_GRP, ROWS // N_GRP, cols), 'grp', 0, 0, til...]
  transfers between devices with their start and end apart: 2 -> 21, of which waited for: 2 -> 7; matrix products, arithmetic and copies ran while one was open for 10% -> 16% of each run, Pallas kernels for 0% -> 21%
where the time goes in v1:
time: 173 us; the launch traced here: 172 us
  Pallas kernels  45.3 us (26%)
  matrix products  41.2 us (24%)
  starting transfers between devices  39.1 us (23%)
  waiting for transfers between devices  21.9 us (13%)
  blocking collectives  12.8 us (7%)
  other arithmetic  5.96 us (3%)
  local copies, waits for them, and re-layouts  4.35 us (3%)
    pallas_call x8, Pallas kernels, call(): pl.pallas_call(body, grid_spec=pltpu.PrefetchScalarGridSpec(num_scalar_pr...  42.5 us
    dot_general x2, matrix products, local(): lax.dot_general(context, out_grad[:, start:start + cols], (((0,), (0,)),...  41.2 us
    ppermute x19, starting transfers between devices, send(): return lax.ppermute(value, ('grp', 'shard'), pairs)  30.7 us
    ppermute x19, waiting for transfers between devices, send(): return lax.ppermute(value, ('grp', 'shard'), pairs)  14.1 us
    all_gather x1, blocking collectives, local(): lax.all_gather(master_new.astype(bf16)[None], 'grp', axis=1, tiled=True)  12.8 us
    all_to_all x2, starting transfers between devices, local(): lax.all_to_all(mine.reshape(N_GRP, ROWS // N_GRP, cols), 'grp', 0, 0, til...  8.44 us
    all_to_all x2, waiting for transfers between devices, local(): lax.all_to_all(mine.reshape(N_GRP, ROWS // N_GRP, cols), 'grp', 0, 0, til...  7.76 us
  transfers between devices with their start and end apart: 21, of which 7 were waited for; matrix products, arithmetic and copies ran while one was open for 16% of the time, Pallas kernels for 21%

profile of v1, /device:TPU:0, one launch (start us, length us, event | category | flops | bytes accessed | tf_op | source)
XLA Modules:
  0.0 171.6 jit_solution(12959575170599725430)
XLA Ops:
  0.8 20.6 %fusion.2.p.p0.p1 = f32[2048,2048]{1,0:T(8,128)} fusion(bf16[1536,2048]{1,0:T(8,128)(2,1)} %param.6, bf16[1536,4096]{1,0:T(8,128)(2,1)} %param.7), kind=kOutput, calls=%fused_computation.2 | convolution fusion | flops 12884901888 | bytes 29360128 | tf_op jit(solution)/shard_map/dot_general | solution.py:220
  21.4 9.6 %for_other_core.2 = bf16[16,64,2048]{2,1,0:T(8,128)(2,1)S(1)} custom-call(s32[32]{0:T(128)S(1)} %pad_add_fusion.1.t, f32[2048,2048]{1,0:T(8,128)} %fusion.2.p.p0.p1), custom_call_target="tpu_custom_call" | custom-call | flops 3145728 | bytes 12582912 | tf_op jit(solution)/shard_map/for_other_core/pallas_call | solution.py:58
  31.3 20.6 %fusion.p.p0.p1 = f32[2048,2048]{1,0:T(8,128)} fusion(bf16[1536,2048]{1,0:T(8,128)(2,1)} %param.6, bf16[1536,4096]{1,0:T(8,128)(2,1)} %param.7), kind=kOutput, calls=%fused_computation | convolution fusion | flops 12884901888 | bytes 29360128 | tf_op jit(solution)/shard_map/dot_general | solution.py:220
  51.9 9.6 %for_other_core.3 = bf16[16,64,2048]{2,1,0:T(8,128)(2,1)S(1)} custom-call(s32[32]{0:T(128)S(1)} %pad_add_fusion.1.t, f32[2048,2048]{1,0:T(8,128)} %fusion.p.p0.p1), custom_call_target="tpu_custom_call" | custom-call | flops 3145728 | bytes 12582912 | tf_op jit(solution)/shard_map/for_other_core/pallas_call | solution.py:58
  62.1 5.6 %first_sends.2 = (bf16[4,64,2048]{2,1,0:T(8,128)(2,1)}, bf16[4,64,2048]{2,1,0:T(8,128)(2,1)}) custom-call(s32[32]{0:T(128)S(1)} %pad_add_fusion.1.t, f32[2048,2048]{1,0:T(8,128)} %fusion.2.p.p0.p1, bf16[16,64,2048]{2,1,0:T(8,128)(2,1)S(1)} %collective-permute-done.3.r0.r1.r, f32[2048,2048]{1,0:T(8,128)} %fusion.2.p.p0.p1, ...), custom_call_target="tpu_custom_call" | custom-call | flops 2097152 | bytes 8388608 | tf_op jit(solution)/shard_map/first_sends/pallas_call | solution.py:58
  67.7 2.8 %collective-permute-start.4 = (bf16[4,64,2048]{2,1,0:T(8,128)(2,1)}, bf16[4,64,2048]{2,1,0:T(8,128)(2,1)S(1)}, u32[]{:S(2)}, u32[]{:S(2)}) collective-permute-start(bf16[4,64,2048]{2,1,0:T(8,128)(2,1)} %get-tuple-element.28), channel_id=1, source_target_pairs={{0,6},{1,25},{2,0},{3,27},{4,2},{5,29},{6,4},{7,31},{8,14},{9,1},{... | collective-permute-start | bytes 3145736 | tf_op jit(solution)/shard_map/ppermute | solution.py:41
  70.5 5.6 %first_sends.3 = (bf16[4,64,2048]{2,1,0:T(8,128)(2,1)}, bf16[4,64,2048]{2,1,0:T(8,128)(2,1)}) custom-call(s32[32]{0:T(128)S(1)} %pad_add_fusion.1.t, f32[2048,2048]{1,0:T(8,128)} %fusion.p.p0.p1, bf16[16,64,2048]{2,1,0:T(8,128)(2,1)S(1)} %collective-permute-done.11.r0.r1.r, f32[2048,2048]{1,0:T(8,128)} %fusion.p.p0.p1, ...), custom_call_target="tpu_custom_call" | custom-call | flops 2097152 | bytes 8388608 | tf_op jit(solution)/shard_map/first_sends/pallas_call | solution.py:58
  76.1 3.2 %collective-permute-start.12 = (bf16[4,64,2048]{2,1,0:T(8,128)(2,1)}, bf16[4,64,2048]{2,1,0:T(8,128)(2,1)S(1)}, u32[]{:S(2)}, u32[]{:S(2)}) collective-permute-start(bf16[4,64,2048]{2,1,0:T(8,128)(2,1)} %get-tuple-element.36), channel_id=1, source_target_pairs={{0,6},{1,25},{2,0},{3,27},{4,2},{5,29},{6,4},{7,31},{8,14},{9,1},{... | collective-permute-start | bytes 3145736 | tf_op jit(solution)/shard_map/ppermute | solution.py:41
  79.5 3.6 %collective-permute-done.4.b.a0 = bf16[4,64,2048]{2,1,0:T(8,128)(2,1)S(1)} collective-permute-done((bf16[4,64,2048]{2,1,0:T(8,128)(2,1)}, bf16[4,64,2048]{2,1,0:T(8,128)(2,1)S(1)}, u32[]{:S(2)}, u32[]{:S(2)}) %collective-permute-start.4) | collective-permute-done | bytes 1048608 | tf_op jit(solution)/shard_map/ppermute | solution.py:41
  83.1 3.7 %collective-permute-done.5.a.a1 = bf16[4,64,2048]{2,1,0:T(8,128)(2,1)} collective-permute-done((bf16[4,64,2048]{2,1,0:T(8,128)(2,1)}, bf16[4,64,2048]{2,1,0:T(8,128)(2,1)}, u32[]{:S(2)}, u32[]{:S(2)}) %collective-permute-start.5) | collective-permute-done | bytes 1048608 | tf_op jit(solution)/shard_map/ppermute | solution.py:41
  91.6 3.2 %collective-permute-start.7 = (bf16[2,64,2048]{2,1,0:T(8,128)(2,1)S(1)}, bf16[2,64,2048]{2,1,0:T(8,128)(2,1)S(1)}, u32[]{:S(2)}, u32[]{:S(2)}) collective-permute-start(bf16[2,64,2048]{2,1,0:T(8,128)(2,1)S(1)} %get-tuple-element.31), channel_id=1, source_target_pairs={{0,6},{1,25},{2,0},{3,27},{4,2},{5,29},{6,4},{7,31},{8,14},{9,1},{... | collective-permute-start | bytes 1572872 | tf_op jit(solution)/shard_map/ppermute | solution.py:41
  95.4 2.6 %collective-permute-done.13.a.a1 = bf16[4,64,2048]{2,1,0:T(8,128)(2,1)S(1)} collective-permute-done((bf16[4,64,2048]{2,1,0:T(8,128)(2,1)}, bf16[4,64,2048]{2,1,0:T(8,128)(2,1)S(1)}, u32[]{:S(2)}, u32[]{:S(2)}) %collective-permute-start.13) | collective-permute-done | bytes 1048608 | tf_op jit(solution)/shard_map/ppermute | solution.py:41
  100.4 3.2 %collective-permute-start.15 = (bf16[2,64,2048]{2,1,0:T(8,128)(2,1)S(1)}, bf16[2,64,2048]{2,1,0:T(8,128)(2,1)S(1)}, u32[]{:S(2)}, u32[]{:S(2)}) collective-permute-start(bf16[2,64,2048]{2,1,0:T(8,128)(2,1)S(1)} %get-tuple-element.39), channel_id=1, source_target_pairs={{0,6},{1,25},{2,0},{3,27},{4,2},{5,29},{6,4},{7,31},{8,14},{9,1},{... | collective-permute-start | bytes 1572872 | tf_op jit(solution)/shard_map/ppermute | solution.py:41
  104.9 3.3 %first_sums.2 = (f32[64,2048]{1,0:T(8,128)S(1)}, bf16[64,2048]{1,0:T(8,128)(2,1)S(1)}, bf16[64,2048]{1,0:T(8,128)(2,1)S(1)}, bf16[64,2048]{1,0:T(8,128)(2,1)S(1)}) custom-call(s32[32]{0:T(128)S(1)} %pad_add_fusion.1.t, f32[2048,2048]{1,0:T(8,128)} %fusion.2.p.p0.p1, bf16[16,64,2048]{2,1,0:T(8,128)(2,1)S(1)} %copy-done.3, ...), custom_call_target="tpu_custom_call" | custom-call | flops 1703936 | bytes 6815744 | tf_op jit(solution)/shard_map/first_sums/pallas_call | solution.py:58
  108.2 3.1 %collective-permute-start.10 = (bf16[64,2048]{1,0:T(8,128)(2,1)S(1)}, bf16[64,2048]{1,0:T(8,128)(2,1)S(1)}, u32[]{:S(2)}, u32[]{:S(2)}) collective-permute-start(bf16[64,2048]{1,0:T(8,128)(2,1)S(1)} %get-tuple-element.35), channel_id=1, source_target_pairs={{0,24},{1,7},{2,26},{3,1},{4,28},{5,3},{6,30},{7,5},{8,0},{9,15},{... | collective-permute-start | bytes 786440 | tf_op jit(solution)/shard_map/ppermute | solution.py:41
  114.4 2.9 %windows.1 = (f32[3,512,128]{2,1,0:T(8,128)S(1)}, bf16[3,512,128]{2,1,0:T(8,128)(2,1)}, bf16[3,512,128]{2,1,0:T(8,128)(2,1)}, bf16[3,512,128]{2,1,0:T(8,128)(2,1)S(1)}) custom-call(s32[13]{0:T(128)S(1)} %pad_add_fusion.s, f32[3,1024,128]{2,1,0:T(8,128)S(1)} %pad_maximum_fusion.piece), custom_call_target="tpu_custom_call" | custom-call | flops 10000000 | bytes 4000000 | tf_op jit(solution)/shard_map/windows/pallas_call | solution.py:195
  119.2 3.5 %collective-permute-start.1 = (bf16[3,512,128]{2,1,0:T(8,128)(2,1)}, bf16[3,512,128]{2,1,0:T(8,128)(2,1)}, u32[]{:S(2)}, u32[]{:S(2)}) collective-permute-start(bf16[3,512,128]{2,1,0:T(8,128)(2,1)} %get-tuple-element.26), channel_id=1, source_target_pairs={{0,64},{1,65},{2,66},{3,67},{4,68},{5,69},{6,70},{7,71},{8,72},{9,... | collective-permute-start | bytes 1179656 | tf_op jit(solution)/shard_map/ppermute | solution.py:41
  122.8 4.1 %first_sums.3 = (f32[64,2048]{1,0:T(8,128)S(1)}, bf16[64,2048]{1,0:T(8,128)(2,1)}, bf16[64,2048]{1,0:T(8,128)(2,1)}, bf16[64,2048]{1,0:T(8,128)(2,1)}) custom-call(s32[32]{0:T(128)S(1)} %pad_add_fusion.1.t, f32[2048,2048]{1,0:T(8,128)} %fusion.p.p0.p1, bf16[16,64,2048]{2,1,0:T(8,128)(2,1)S(1)} %copy-done.1, ...), custom_call_target="tpu_custom_call" | custom-call | flops 1703936 | bytes 6815744 | tf_op jit(solution)/shard_map/first_sums/pallas_call | solution.py:58
  132.4 3.5 %all-to-all-start = ((f32[4,16,2048]{2,1,0:T(8,128)}), f32[4,16,2048]{2,1,0:T(8,128)S(1)}, u32[]{:S(2)}, u32[]{:S(2)}) async-start(f32[4,16,2048]{2,1,0:T(8,128)} %bitcast.8), calls=%async_computation | async-start | bytes 1048576 | tf_op jit(solution)/shard_map/all_to_all | solution.py:232
  140.1 3.9 %all-to-all-done = f32[4,16,2048]{2,1,0:T(8,128)S(1)} async-done(((f32[4,16,2048]{2,1,0:T(8,128)}), f32[4,16,2048]{2,1,0:T(8,128)S(1)}, u32[]{:S(2)}, u32[]{:S(2)}) %all-to-all-start) | async-done | bytes 524320 | tf_op jit(solution)/shard_map/all_to_all | solution.py:232
  144.0 5.0 %all-to-all-start.1 = ((f32[4,16,2048]{2,1,0:T(8,128)}), f32[4,16,2048]{2,1,0:T(8,128)S(1)}, u32[]{:S(2)}, u32[]{:S(2)}) async-start(f32[4,16,2048]{2,1,0:T(8,128)} %bitcast.10), calls=%async_computation.1 | async-start | bytes 1048576 | tf_op jit(solution)/shard_map/all_to_all | solution.py:232
  149.0 2.6 %collective-permute-done.2 = bf16[3,512,128]{2,1,0:T(8,128)(2,1)S(1)} collective-permute-done((bf16[3,512,128]{2,1,0:T(8,128)(2,1)}, bf16[3,512,128]{2,1,0:T(8,128)(2,1)S(1)}, u32[]{:S(2)}, u32[]{:S(2)}) %collective-permute-start.2) | collective-permute-done | bytes 393248 | tf_op jit(solution)/shard_map/ppermute | solution.py:41
  153.2 3.8 %all-to-all-done.1 = f32[4,16,2048]{2,1,0:T(8,128)S(1)} async-done(((f32[4,16,2048]{2,1,0:T(8,128)}), f32[4,16,2048]{2,1,0:T(8,128)S(1)}, u32[]{:S(2)}, u32[]{:S(2)}) %all-to-all-start.1) | async-done | bytes 524320 | tf_op jit(solution)/shard_map/all_to_all | solution.py:232
  158.0 12.8 %all_gather.3 = bf16[1,64,4096]{2,1,0:T(8,128)(2,1)S(1)} all-gather(bf16[1,16,4096]{2,1,0:T(8,128)(2,1)S(1)} %get-tuple-element.44), channel_id=1, replica_groups=mesh['grp'=4,'shard'=32] {'grp'}, dimensions={1}, use_global_device_ids=true | all-gather | bytes 655360 | tf_op jit(solution)/shard_map/all_gather | solution.py:243
  (69 shorter events, 28.2 us)
Async XLA Ops:
  31.0 31.1 %collective-permute-start.3 = (bf16[16,64,2048]{2,1,0:T(8,128)(2,1)S(1)}, bf16[16,64,2048]{2,1,0:T(8,128)(2,1)S(1)}, u32[]{:S(2)}, u32[]{:S(2)}) collective-permute-start(bf16[16,64,2048]{2,1,0:T(8,128)(2,1)S(1)} %for_other_core.2), channel_id=1, source_target_pairs={{0,1},{1,0},{2,3},{3,2},{4,5},{5,4},{6,7},{7,6},{8,9},{9,8},{10,11... | collective-permute-start | bytes 12582920 | tf_op jit(solution)/shard_map/ppermute | solution.py:41
  61.5 9.0 %collective-permute-start.11 = (bf16[16,64,2048]{2,1,0:T(8,128)(2,1)S(1)}, bf16[16,64,2048]{2,1,0:T(8,128)(2,1)S(1)}, u32[]{:S(2)}, u32[]{:S(2)}) collective-permute-start(bf16[16,64,2048]{2,1,0:T(8,128)(2,1)S(1)} %for_other_core.3), channel_id=1, source_target_pairs={{0,1},{1,0},{2,3},{3,2},{4,5},{5,4},{6,7},{7,6},{8,9},{9,8},{10,11... | collective-permute-start | bytes 12582920 | tf_op jit(solution)/shard_map/ppermute | solution.py:41
  67.7 15.5 %collective-permute-start.4 = (bf16[4,64,2048]{2,1,0:T(8,128)(2,1)}, bf16[4,64,2048]{2,1,0:T(8,128)(2,1)S(1)}, u32[]{:S(2)}, u32[]{:S(2)}) collective-permute-start(bf16[4,64,2048]{2,1,0:T(8,128)(2,1)} %get-tuple-element.28), channel_id=1, source_target_pairs={{0,6},{1,25},{2,0},{3,27},{4,2},{5,29},{6,4},{7,31},{8,14},{9,1},{... | collective-permute-start | bytes 3145736 | tf_op jit(solution)/shard_map/ppermute | solution.py:41
  70.5 16.3 %collective-permute-start.5 = (bf16[4,64,2048]{2,1,0:T(8,128)(2,1)}, bf16[4,64,2048]{2,1,0:T(8,128)(2,1)}, u32[]{:S(2)}, u32[]{:S(2)}) collective-permute-start(bf16[4,64,2048]{2,1,0:T(8,128)(2,1)} %get-tuple-element.29), channel_id=1, source_target_pairs={{0,2},{1,9},{2,4},{3,11},{4,6},{5,13},{6,0},{7,15},{8,10},{9,17},{... | collective-permute-start | bytes 3145736 | tf_op jit(solution)/shard_map/ppermute | solution.py:41
  76.1 19.3 %collective-permute-start.12 = (bf16[4,64,2048]{2,1,0:T(8,128)(2,1)}, bf16[4,64,2048]{2,1,0:T(8,128)(2,1)S(1)}, u32[]{:S(2)}, u32[]{:S(2)}) collective-permute-start(bf16[4,64,2048]{2,1,0:T(8,128)(2,1)} %get-tuple-element.36), channel_id=1, source_target_pairs={{0,6},{1,25},{2,0},{3,27},{4,2},{5,29},{6,4},{7,31},{8,14},{9,1},{... | collective-permute-start | bytes 3145736 | tf_op jit(solution)/shard_map/ppermute | solution.py:41
  79.3 18.6 %collective-permute-start.13 = (bf16[4,64,2048]{2,1,0:T(8,128)(2,1)}, bf16[4,64,2048]{2,1,0:T(8,128)(2,1)S(1)}, u32[]{:S(2)}, u32[]{:S(2)}) collective-permute-start(bf16[4,64,2048]{2,1,0:T(8,128)(2,1)} %get-tuple-element.37), channel_id=1, source_target_pairs={{0,2},{1,9},{2,4},{3,11},{4,6},{5,13},{6,0},{7,15},{8,10},{9,17},{... | collective-permute-start | bytes 3145736 | tf_op jit(solution)/shard_map/ppermute | solution.py:41
  79.5 18.5 %copy-start.1 = (bf16[16,64,2048]{2,1,0:T(8,128)(2,1)S(1)}, bf16[16,64,2048]{2,1,0:T(8,128)(2,1)}, u32[]{:S(2)}) copy-start(bf16[16,64,2048]{2,1,0:T(8,128)(2,1)} %copy-done) | copy-start | bytes 12582916
  91.5 13.4 %collective-permute-start.6 = (bf16[2,64,2048]{2,1,0:T(8,128)(2,1)S(1)}, bf16[2,64,2048]{2,1,0:T(8,128)(2,1)S(1)}, u32[]{:S(2)}, u32[]{:S(2)}) collective-permute-start(bf16[2,64,2048]{2,1,0:T(8,128)(2,1)S(1)} %get-tuple-element.30), channel_id=1, source_target_pairs={{0,2},{1,9},{2,4},{3,11},{4,6},{5,13},{6,0},{7,15},{8,10},{9,17},{... | collective-permute-start | bytes 1572872 | tf_op jit(solution)/shard_map/ppermute | solution.py:41
  91.6 13.3 %collective-permute-start.7 = (bf16[2,64,2048]{2,1,0:T(8,128)(2,1)S(1)}, bf16[2,64,2048]{2,1,0:T(8,128)(2,1)S(1)}, u32[]{:S(2)}, u32[]{:S(2)}) collective-permute-start(bf16[2,64,2048]{2,1,0:T(8,128)(2,1)S(1)} %get-tuple-element.31), channel_id=1, source_target_pairs={{0,6},{1,25},{2,0},{3,27},{4,2},{5,29},{6,4},{7,31},{8,14},{9,1},{... | collective-permute-start | bytes 1572872 | tf_op jit(solution)/shard_map/ppermute | solution.py:41
  100.3 17.0 %collective-permute-start.14 = (bf16[2,64,2048]{2,1,0:T(8,128)(2,1)S(1)}, bf16[2,64,2048]{2,1,0:T(8,128)(2,1)S(1)}, u32[]{:S(2)}, u32[]{:S(2)}) collective-permute-start(bf16[2,64,2048]{2,1,0:T(8,128)(2,1)S(1)} %get-tuple-element.38), channel_id=1, source_target_pairs={{0,2},{1,9},{2,4},{3,11},{4,6},{5,13},{6,0},{7,15},{8,10},{9,17},{... | collective-permute-start | bytes 1572872 | tf_op jit(solution)/shard_map/ppermute | solution.py:41
  100.4 18.9 %collective-permute-start.15 = (bf16[2,64,2048]{2,1,0:T(8,128)(2,1)S(1)}, bf16[2,64,2048]{2,1,0:T(8,128)(2,1)S(1)}, u32[]{:S(2)}, u32[]{:S(2)}) collective-permute-start(bf16[2,64,2048]{2,1,0:T(8,128)(2,1)S(1)} %get-tuple-element.39), channel_id=1, source_target_pairs={{0,6},{1,25},{2,0},{3,27},{4,2},{5,29},{6,4},{7,31},{8,14},{9,1},{... | collective-permute-start | bytes 1572872 | tf_op jit(solution)/shard_map/ppermute | solution.py:41
  104.9 9.4 %copy-start.6 = (f32[1,1,131072]{2,1,0:T(1,128)S(1)}, f32[1,1,131072]{2,1,0:T(1,128)}, u32[]{:S(2)}) copy-start(f32[1,1,131072]{2,1,0:T(1,128)} %param.9) | copy-start | bytes 1572868
  108.2 18.6 %collective-permute-start.10 = (bf16[64,2048]{1,0:T(8,128)(2,1)S(1)}, bf16[64,2048]{1,0:T(8,128)(2,1)S(1)}, u32[]{:S(2)}, u32[]{:S(2)}) collective-permute-start(bf16[64,2048]{1,0:T(8,128)(2,1)S(1)} %get-tuple-element.35), channel_id=1, source_target_pairs={{0,24},{1,7},{2,26},{3,1},{4,28},{5,3},{6,30},{7,5},{8,0},{9,15},{... | collective-permute-start | bytes 786440 | tf_op jit(solution)/shard_map/ppermute | solution.py:41
  111.3 17.4 %collective-permute-start.8 = (bf16[64,2048]{1,0:T(8,128)(2,1)S(1)}, bf16[64,2048]{1,0:T(8,128)(2,1)S(1)}, u32[]{:S(2)}, u32[]{:S(2)}) collective-permute-start(bf16[64,2048]{1,0:T(8,128)(2,1)S(1)} %get-tuple-element.33), channel_id=1, source_target_pairs={{0,8},{1,3},{2,10},{3,5},{4,12},{5,7},{6,14},{7,1},{8,16},{9,11},{... | collective-permute-start | bytes 786440 | tf_op jit(solution)/shard_map/ppermute | solution.py:41
  111.3 18.1 %collective-permute-start.9 = (bf16[64,2048]{1,0:T(8,128)(2,1)S(1)}, bf16[64,2048]{1,0:T(8,128)(2,1)S(1)}, u32[]{:S(2)}, u32[]{:S(2)}) collective-permute-start(bf16[64,2048]{1,0:T(8,128)(2,1)S(1)} %get-tuple-element.34), channel_id=1, source_target_pairs={{0,16},{1,5},{2,18},{3,7},{4,20},{5,1},{6,22},{7,3},{8,24},{9,13},... | collective-permute-start | bytes 786440 | tf_op jit(solution)/shard_map/ppermute | solution.py:41
  117.2 9.6 %copy-start.4 = (bf16[3,512,128]{2,1,0:T(8,128)(2,1)}, bf16[3,512,128]{2,1,0:T(8,128)(2,1)S(1)}, u32[]{:S(2)}) copy-start(bf16[3,512,128]{2,1,0:T(8,128)(2,1)S(1)} %get-tuple-element.27) | copy-start | bytes 1179652
  117.2 31.7 %collective-permute-start = (bf16[3,512,128]{2,1,0:T(8,128)(2,1)}, bf16[3,512,128]{2,1,0:T(8,128)(2,1)}, u32[]{:S(2)}, u32[]{:S(2)}) collective-permute-start(bf16[3,512,128]{2,1,0:T(8,128)(2,1)} %get-tuple-element.25), channel_id=1, source_target_pairs={{0,32},{1,33},{2,34},{3,35},{4,36},{5,37},{6,38},{7,39},{8,40},{9,... | collective-permute-start | bytes 1179656 | tf_op jit(solution)/shard_map/ppermute | solution.py:41
  119.2 29.7 %collective-permute-start.1 = (bf16[3,512,128]{2,1,0:T(8,128)(2,1)}, bf16[3,512,128]{2,1,0:T(8,128)(2,1)}, u32[]{:S(2)}, u32[]{:S(2)}) collective-permute-start(bf16[3,512,128]{2,1,0:T(8,128)(2,1)} %get-tuple-element.26), channel_id=1, source_target_pairs={{0,64},{1,65},{2,66},{3,67},{4,68},{5,69},{6,70},{7,71},{8,72},{9,... | collective-permute-start | bytes 1179656 | tf_op jit(solution)/shard_map/ppermute | solution.py:41
  126.8 10.6 %collective-permute-start.16 = (bf16[64,2048]{1,0:T(8,128)(2,1)}, bf16[64,2048]{1,0:T(8,128)(2,1)S(1)}, u32[]{:S(2)}, u32[]{:S(2)}) collective-permute-start(bf16[64,2048]{1,0:T(8,128)(2,1)} %get-tuple-element.41), channel_id=1, source_target_pairs={{0,8},{1,3},{2,10},{3,5},{4,12},{5,7},{6,14},{7,1},{8,16},{9,11},{... | collective-permute-start | bytes 786440 | tf_op jit(solution)/shard_map/ppermute | solution.py:41
  128.8 10.4 %collective-permute-start.17 = (bf16[64,2048]{1,0:T(8,128)(2,1)}, bf16[64,2048]{1,0:T(8,128)(2,1)S(1)}, u32[]{:S(2)}, u32[]{:S(2)}) collective-permute-start(bf16[64,2048]{1,0:T(8,128)(2,1)} %get-tuple-element.42), channel_id=1, source_target_pairs={{0,16},{1,5},{2,18},{3,7},{4,20},{5,1},{6,22},{7,3},{8,24},{9,13},... | collective-permute-start | bytes 786440 | tf_op jit(solution)/shard_map/ppermute | solution.py:41
  129.4 9.7 %collective-permute-start.18 = (bf16[64,2048]{1,0:T(8,128)(2,1)}, bf16[64,2048]{1,0:T(8,128)(2,1)S(1)}, u32[]{:S(2)}, u32[]{:S(2)}) collective-permute-start(bf16[64,2048]{1,0:T(8,128)(2,1)} %get-tuple-element.43), channel_id=1, source_target_pairs={{0,24},{1,7},{2,26},{3,1},{4,28},{5,3},{6,30},{7,5},{8,0},{9,15},{... | collective-permute-start | bytes 786440 | tf_op jit(solution)/shard_map/ppermute | solution.py:41
  132.4 11.5 %all-to-all-start = ((f32[4,16,2048]{2,1,0:T(8,128)}), f32[4,16,2048]{2,1,0:T(8,128)S(1)}, u32[]{:S(2)}, u32[]{:S(2)}) async-start(f32[4,16,2048]{2,1,0:T(8,128)} %bitcast.8), calls=%async_computation | async-start | bytes 1048576 | tf_op jit(solution)/shard_map/all_to_all | solution.py:232
  137.5 14.1 %collective-permute-start.2 = (bf16[3,512,128]{2,1,0:T(8,128)(2,1)}, bf16[3,512,128]{2,1,0:T(8,128)(2,1)S(1)}, u32[]{:S(2)}, u32[]{:S(2)}) collective-permute-start(bf16[3,512,128]{2,1,0:T(8,128)(2,1)} %copy-done.4), channel_id=1, source_target_pairs={{0,96},{1,97},{2,98},{3,99},{4,100},{5,101},{6,102},{7,103},{8,104... | collective-permute-start | bytes 1179656 | tf_op jit(solution)/shard_map/ppermute | solution.py:41
  144.0 13.1 %all-to-all-start.1 = ((f32[4,16,2048]{2,1,0:T(8,128)}), f32[4,16,2048]{2,1,0:T(8,128)S(1)}, u32[]{:S(2)}, u32[]{:S(2)}) async-start(f32[4,16,2048]{2,1,0:T(8,128)} %bitcast.10), calls=%async_computation.1 | async-start | bytes 1048576 | tf_op jit(solution)/shard_map/all_to_all | solution.py:232
  (6 other events, 41.0 us)

commit v2 on v0

v2 whole, which is shorter than its diff:
```python
import jax
import jax.numpy as jnp
from jax import lax
from jax.experimental import pallas as pl
from jax.experimental.pallas import tpu as pltpu
from jax.sharding import PartitionSpec as P

beta_one = 0.9
beta_two = 0.95
step_size = 0.01
epsilon = 1e-08

N_GRP = 4
ROWS = 64
CHUNKS = (2048, 2048)
TILE = 512
f32, bf16 = jnp.float32, jnp.bfloat16
AXES = ("grp", "shard")

DEVICES = [(z, y, x, c) for z in range(4) for y in range(4) for x in range(4) for c in range(2)]
SWAP = [(i, i ^ 1) for i in range(128)]


def number(z, y, x, c):
    return (((z % 4) * 4 + y % 4) * 4 + x % 4) * 2 + c


FIRST = {
    k: [(number(z, y, x, c), number(z, y + k * c, x + k * (1 - c), c)) for z, y, x, c in DEVICES] for k in (1, 2, 3)
}


def grouped(key, order):
    groups = {}
    for place in sorted(DEVICES, key=lambda place: order(*place)):
        groups.setdefault(key(*place), []).append(number(*place))
    return list(groups.values())


SECOND = grouped(lambda z, y, x, c: (c, y if c else x), lambda z, y, x, c: (y, x, z))


def row_table(shard):
    core, x, y = shard % 2, (shard // 2) % 4, shard // 8

    def of(c):
        i = jnp.arange(16, dtype=jnp.int32)
        ahead, second = i // 4, i % 4
        return 2 * jnp.where(c == 0, second * 4 + (x + ahead) % 4, (y + ahead) % 4 * 4 + second) + c

    return jnp.concatenate([of(core), of(1 - core)]).astype(jnp.int32)


def params():
    return pltpu.CompilerParams(vmem_limit_bytes=60 * 2**20)


def cost(tokens, height, cols):
    return pl.CostEstimate(
        flops=2 * tokens * height * cols // 16, bytes_accessed=(tokens + height) * cols // 8, transcendentals=0
    )


def product(left, right):
    return lax.dot_general(left, right, (((0,), (0,)), ((), ())), preferred_element_type=f32)


def first_product(table, context, out_grad, start, cols):
    tokens, height = context.shape
    half, parts = height // 2, 4
    slab = tokens // parts

    def body(t, c_hbm, g, out, mine_hbm, other_hbm, c, mine, other, arrived, left):
        step = pl.program_id(0)

        def piece(m):
            at = pl.ds(m * slab, slab)
            return pltpu.make_async_copy(c_hbm.at[at], c.at[at], arrived.at[m])

        def away():
            return [
                pltpu.make_async_copy(mine, mine_hbm, left.at[0]),
                pltpu.make_async_copy(other, other_hbm, left.at[1]),
            ]

        def choose(to, base, core):
            for m in range(parts):
                at = pl.ds(m * slab, slab)
                for k in range(8):
                    low, high = [
                        c[at, pl.ds(pl.multiple_of((t[base + 2 * k + i] >> 1) * 128, 128), 128)] for i in (0, 1)
                    ]
                    to[at, pl.ds(k * 128, 128)] = jnp.concatenate(
                        [low[:, core * 64:core * 64 + 64], high[:, core * 64:core * 64 + 64]], axis=1
                    )

        @pl.when(step == 0)
        def _():
            for m in range(parts):
                piece(m).start()
            for m in range(parts):
                piece(m).wait()

            @pl.when((t[0] & 1) == 0)
            def _():
                choose(other, 16, 1)
                choose(mine, 0, 0)

            @pl.when((t[0] & 1) == 1)
            def _():
                choose(other, 16, 0)
                choose(mine, 0, 1)

            for copy in away():
                copy.start()

        out[...] = product(other[...], g[...]).astype(bf16)

        @pl.when(step == cols // TILE - 1)
        def _():
            for copy in away():
                copy.wait()

    hbm = pl.BlockSpec(memory_space=pl.ANY)
    return pl.pallas_call(
        body,
        grid_spec=pltpu.PrefetchScalarGridSpec(
            num_scalar_prefetch=1,
            grid=(cols // TILE,),
            in_specs=[hbm, pl.BlockSpec((tokens, TILE), lambda i, t: (0, start // TILE + i))],
            out_specs=[pl.BlockSpec((half, TILE), lambda i, t: (0, i)), hbm, hbm],
            scratch_shapes=[
                pltpu.VMEM((tokens, height), bf16),
                pltpu.VMEM((tokens, half), bf16),
                pltpu.VMEM((tokens, half), bf16),
                pltpu.SemaphoreType.DMA((parts,)),
                pltpu.SemaphoreType.DMA((2,)),
            ],
        ),
        out_shape=[
            jax.ShapeDtypeStruct((half, cols), bf16),
            jax.ShapeDtypeStruct((tokens, half), bf16),
            jax.ShapeDtypeStruct((tokens, half), bf16),
        ],
        name="first_product",
        cost_estimate=cost(tokens, half, cols),
        compiler_params=params(),
    )(table, context, out_grad)


def other_product(other, out_grad, start, cols):
    tokens, half = other.shape

    def body(c, g, out):
        out[...] = product(c[...], g[...]).astype(bf16)

    return pl.pallas_call(
        body,
        grid=(cols // TILE,),
        in_specs=[
            pl.BlockSpec((tokens, half), lambda i: (0, 0), pipeline_mode=pl.Buffered(1)),
            pl.BlockSpec((tokens, TILE), lambda i: (0, start // TILE + i)),
        ],
        out_specs=pl.BlockSpec((half, TILE), lambda i: (0, i)),
        out_shape=jax.ShapeDtypeStruct((half, cols), bf16),
        name="other_product",
        cost_estimate=cost(tokens, half, cols),
        compiler_params=params(),
    )(other, out_grad)


def chip_product(mine, out_grad, received, start, cols):
    tokens, half = mine.shape
    quarter = half // 4

    def body(c, g, r, own, *away):
        total = product(c[...], g[...]) + r[...].astype(f32)
        own[...] = total[:quarter]
        for k in range(3):
            away[k][...] = total[(k + 1) * quarter:(k + 2) * quarter].astype(bf16)

    return pl.pallas_call(
        body,
        grid=(cols // TILE,),
        in_specs=[
            pl.BlockSpec((tokens, half), lambda i: (0, 0), pipeline_mode=pl.Buffered(1)),
            pl.BlockSpec((tokens, TILE), lambda i: (0, start // TILE + i)),
            pl.BlockSpec((half, TILE), lambda i: (0, i)),
        ],
        out_specs=[pl.BlockSpec((quarter, TILE), lambda i: (0, i))] * 4,
        out_shape=[jax.ShapeDtypeStruct((quarter, cols), f32)] + [jax.ShapeDtypeStruct((quarter, cols), bf16)] * 3,
        name="chip_product",
        cost_estimate=cost(tokens, half, cols),
        compiler_params=params(),
    )(mine, out_grad, received)


def windows(lengths, pieces):
    cap = pieces[0].size
    n, rows = cap // 256, cap // 128

    def body(s, p0, p1, p2, out, held):
        group = s[N_GRP]
        begin = jnp.int32(0)
        for k in range(N_GRP):
            begin = begin + jnp.where(k < group, s[k], 0)
        length = s[group]
        lane = lax.broadcasted_iota(jnp.int32, (n, 128), 1)
        at = lax.broadcasted_iota(jnp.int32, (n, 128), 0) * 128 + lane
        for k, piece in enumerate((p0, p1, p2)):
            held[pl.ds(n, rows), :] = piece[...]
            for target in range(N_GRP):
                offset = target * n * 128 - begin
                first = jnp.clip(offset >> 7, -n, rows) + n
                turn = offset & 127
                back = (128 - turn) & 127
                low = pltpu.roll(held[pl.ds(first, n), :], back, 1)
                high = pltpu.roll(held[pl.ds(first + 1, n), :], back, 1)
                value = jnp.where(lane < 128 - turn, low, high)
                inside = (at + offset >= 0) & (at + offset < length)
                out[target, k] = jnp.where(inside, value, 0.0).astype(bf16)

    whole = pl.BlockSpec((rows, 128), lambda i, s: (0, 0))
    return pl.pallas_call(
        body,
        grid_spec=pltpu.PrefetchScalarGridSpec(
            num_scalar_prefetch=1,
            grid=(1,),
            in_specs=[whole] * 3,
            out_specs=pl.BlockSpec((N_GRP, 3, n, 128), lambda i, s: (0, 0, 0, 0)),
            scratch_shapes=[pltpu.VMEM((rows + 2 * n + 8, 128), f32)],
        ),
        out_shape=jax.ShapeDtypeStruct((N_GRP, 3, n, 128), bf16),
        name="windows",
        cost_estimate=pl.CostEstimate(flops=10**7, bytes_accessed=4 * 10**6, transcendentals=0),
        compiler_params=params(),
    )(lengths, *[a.reshape(rows, 128) for a in pieces])


def local(context, out_grad, old_master, old_mom1, old_mom2, old_lengths):
    width = out_grad.shape[1]
    table = row_table(lax.axis_index("shard"))
    scalars = jnp.concatenate([old_lengths[0], lax.axis_index("grp")[None]]).astype(jnp.int32)
    pieces = (old_master, old_mom1, old_mom2)

    first_cols, second_cols = CHUNKS
    theirs, mine, other = first_product(table, context, out_grad, 0, first_cols)
    received = lax.ppermute(theirs, AXES, SWAP)
    theirs = other_product(other, out_grad, first_cols, second_cols)
    received_later = lax.ppermute(theirs, AXES, SWAP)
    (received, mine), theirs = lax.optimization_barrier(((received, mine), theirs))
    own, *away = chip_product(mine, out_grad, received, 0, first_cols)
    (own, away), pieces, mine = lax.optimization_barrier(((own, away), pieces, mine))
    arrived = [lax.ppermute(away[k - 1], AXES, FIRST[k]) for k in (1, 2, 3)]
    cut = windows(scalars, pieces)
    cut, mine = lax.optimization_barrier((cut, mine))
    state = lax.all_to_all(cut, "grp", 0, 0, tiled=True)
    own_later, *away = chip_product(mine, out_grad, received_later, first_cols, second_cols)
    arrived, own_later = lax.optimization_barrier((arrived, own_later))
    arrived_later = [lax.ppermute(away[k - 1], AXES, FIRST[k]) for k in (1, 2, 3)]
    columns = [(0, first_cols, own, arrived), (first_cols, second_cols, own_later, arrived_later)]
    state = jnp.sum(state.astype(f32), axis=0).reshape(3, ROWS // N_GRP, width)

    results = []
    for start, cols, own, arrived in columns:
        summed = own
        for value in arrived:
            summed = summed + value.astype(f32)
        summed = summed.astype(bf16).reshape(16, ROWS // N_GRP, cols)
        summed = lax.all_to_all(summed, AXES, 0, 0, axis_index_groups=SECOND, tiled=True)
        gradient = jnp.sum(summed.astype(f32), axis=0)
        master, first, second = state[:, :, start:start + cols]
        first_new = beta_one * first + (1.0 - beta_one) * gradient
        second_new = beta_two * second + (1.0 - beta_two) * gradient * gradient
        master_new = master - step_size * first_new / (jnp.sqrt(second_new) + epsilon)
        results.append((master_new, first_new, second_new))
    master_new, first_new, second_new = [jnp.concatenate(parts, axis=1) for parts in zip(*results)]
    weights = jnp.broadcast_to(master_new.astype(bf16)[None], (N_GRP,) + master_new.shape)
    weights = lax.all_to_all(weights, "grp", 0, 0, tiled=True).reshape(ROWS, width)
    return (master_new[None], first_new[None], second_new[None], weights[None])


def solution(mesh):
    placed = (
        P(("grp", "shard"), None),
        P(("grp", "shard"), None),
        P("shard", "grp", None),
        P("shard", "grp", None),
        P("shard", "grp", None),
        P("shard", None),
    )
    return jax.shard_map(
        local,
        mesh=mesh,
        in_specs=placed,
        out_specs=(
            P("shard", "grp", None),
            P("shard", "grp", None),
            P("shard", "grp", None),
            P("shard", None, None),
        ),
        check_vma=False,
    )
```

time: 777 us -> 143 us (0.18)
  waiting for transfers between devices: 657 us -> 40.9 us
  Pallas kernels: 0 us -> 54.7 us
  local copies, waits for them, and re-layouts: 35.7 us -> 1.77 us
  matrix products: 32.4 us -> 0 us
  starting transfers between devices: 0.08 us -> 30.6 us
  between operations: 23.2 us -> 0.78 us
  blocking collectives: 12.8 us -> 0 us
    reduce_scatter x1 -> x0, waiting for transfers between devices: 620 us -> none  [local(): lax.psum_scatter(contract(ordered, out_grad), ('grp', 'shard'), scatter_d...]
    pallas_call x0 -> x5, Pallas kernels: none -> 54.7 us  [the longest x2 22.6 us: chip_product(): pl.pallas_call(body, grid=(cols // TILE,), in_specs=[pl.BlockSpec((tokens...]
    all_gather x1 -> x0, waiting for transfers between devices: 37.2 us -> none  [local(): gathered = lax.all_gather(stacked[None], 'grp', axis=0, tiled=True)]
    dot_general x1 -> x0, matrix products: 32.4 us -> none  [contract(): lax.dot_general(columns, out_grad, (((0,), (0,)), ((), ())), preferred_el...]
    slice x3 -> x0, local copies, waits for them, and re-layouts: 22 us -> none  [the longest x1 20.8 us: local(): padded[source]]
    all_to_all x0 -> x4, starting transfers between devices: none -> 21.5 us  [the longest x2 12.7 us: local(): lax.all_to_all(summed, AXES, 0, 0, axis_index_groups=SECOND, tiled=True)]
    all_to_all x0 -> x4, waiting for transfers between devices: none -> 21.4 us  [the longest x2 13.1 us: local(): lax.all_to_all(summed, AXES, 0, 0, axis_index_groups=SECOND, tiled=True)]
    ppermute x0 -> x8, waiting for transfers between devices: none -> 19.5 us  [the longest x3 19.5 us: local(): lax.ppermute(away[k - 1], AXES, FIRST[k])]
  transfers between devices with their start and end apart: 2 -> 12, of which waited for: 2 -> 6; matrix products, arithmetic and copies ran while one was open for 10% -> 8% of each run, Pallas kernels for 0% -> 27%
where the time goes in v2:
time: 143 us; the launch traced here: 142 us
  Pallas kernels  54.7 us (38%)
  waiting for transfers between devices  40.9 us (29%)
  starting transfers between devices  30.6 us (21%)
  other arithmetic  13.4 us (9%)
  local copies, waits for them, and re-layouts  1.77 us (1%)
    pallas_call x2, Pallas kernels, chip_product(): pl.pallas_call(body, grid=(cols // TILE,), in_specs=[pl.BlockSpec((tokens...  22.6 us
    ppermute x3, waiting for transfers between devices, local(): lax.ppermute(away[k - 1], AXES, FIRST[k])  19.5 us
    pallas_call x1, Pallas kernels, first_product(): pl.pallas_call(body, grid_spec=pltpu.PrefetchScalarGridSpec(num_scalar_pr...  16.9 us
    all_to_all x2, waiting for transfers between devices, local(): lax.all_to_all(summed, AXES, 0, 0, axis_index_groups=SECOND, tiled=True)  13.1 us
    all_to_all x2, starting transfers between devices, local(): lax.all_to_all(summed, AXES, 0, 0, axis_index_groups=SECOND, tiled=True)  12.7 us
    pallas_call x1, Pallas kernels, other_product(): pl.pallas_call(body, grid=(cols // TILE,), in_specs=[pl.BlockSpec((tokens...  10.8 us
    convert_element_type x2, other arithmetic, local(): summed = summed.astype(bf16).reshape(16, ROWS // N_GRP, cols)  7.96 us
    all_to_all x1, waiting for transfers between devices, local(): lax.all_to_all(weights, 'grp', 0, 0, tiled=True).reshape(ROWS, width)  5.89 us
  transfers between devices with their start and end apart: 12, of which 6 were waited for; matrix products, arithmetic and copies ran while one was open for 8% of the time, Pallas kernels for 27%

profile of v2, /device:TPU:0, one launch (start us, length us, event | category | flops | bytes accessed | tf_op | source)
XLA Modules:
  0.0 142.2 jit_solution(7122856127532766513)
XLA Ops:
  1.3 16.9 %first_product.1 = (bf16[1024,2048]{1,0:T(8,128)(2,1)}, bf16[1536,1024]{1,0:T(8,128)(2,1)}, bf16[1536,1024]{1,0:T(8,128)(2,1)}) custom-call(s32[32]{0:T(128)} %pad_add_fusion.1.t, bf16[1536,2048]{1,0:T(8,128)(2,1)} %c_hbm.1, bf16[1536,4096]{1,0:T(8,128)(2,1)} %g.7), custom_call_target="tpu_custom_call" | custom-call | flops 402653184 | bytes 655360 | tf_op jit(solution)/shard_map/first_product/pallas_call | solution.py:125
  18.2 10.8 %other_product.1 = bf16[1024,2048]{1,0:T(8,128)(2,1)} custom-call(bf16[1536,1024]{1,0:T(8,128)(2,1)} %get-tuple-element.33.c, bf16[1536,4096]{1,0:T(8,128)(2,1)} %g.7), custom_call_target="tpu_custom_call" | custom-call | flops 402653184 | bytes 655360 | tf_op jit(solution)/shard_map/other_product/pallas_call | solution.py:157
  29.5 11.3 %chip_product.2 = (f32[256,2048]{1,0:T(8,128)}, bf16[256,2048]{1,0:T(8,128)(2,1)}, bf16[256,2048]{1,0:T(8,128)(2,1)}, bf16[256,2048]{1,0:T(8,128)(2,1)}) custom-call(bf16[1536,1024]{1,0:T(8,128)(2,1)} %get-tuple-element.49.c, bf16[1536,4096]{1,0:T(8,128)(2,1)} %g.7, bf16[1024,2048]{1,0:T(8,128)(2,1)} %collective-permute-done.r), custom_call_target="tpu_custom_call" | custom-call | flops 402653184 | bytes 655360 | tf_op jit(solution)/shard_map/chip_product/pallas_call | solution.py:182
  40.8 1.7 %collective-permute-start.1 = (bf16[256,2048]{1,0:T(8,128)(2,1)}, bf16[256,2048]{1,0:T(8,128)(2,1)S(1)}, u32[]{:S(2)}, u32[]{:S(2)}) collective-permute-start(bf16[256,2048]{1,0:T(8,128)(2,1)} %get-tuple-element.46), channel_id=1, source_target_pairs={{0,2},{1,9},{2,4},{3,11},{4,6},{5,13},{6,0},{7,15},{8,10},{9,17},{... | collective-permute-start | bytes 3145736 | tf_op jit(solution)/shard_map/ppermute | solution.py:254
  42.5 2.7 %collective-permute-start.2 = (bf16[256,2048]{1,0:T(8,128)(2,1)}, bf16[256,2048]{1,0:T(8,128)(2,1)}, u32[]{:S(2)}, u32[]{:S(2)}) collective-permute-start(bf16[256,2048]{1,0:T(8,128)(2,1)} %get-tuple-element.47), channel_id=1, source_target_pairs={{0,4},{1,17},{2,6},{3,19},{4,0},{5,21},{6,2},{7,23},{8,12},{9,25},... | collective-permute-start | bytes 3145736 | tf_op jit(solution)/shard_map/ppermute | solution.py:254
  45.2 1.4 %collective-permute-start.3 = (bf16[256,2048]{1,0:T(8,128)(2,1)}, bf16[256,2048]{1,0:T(8,128)(2,1)}, u32[]{:S(2)}, u32[]{:S(2)}) collective-permute-start(bf16[256,2048]{1,0:T(8,128)(2,1)} %get-tuple-element.48), channel_id=1, source_target_pairs={{0,6},{1,25},{2,0},{3,27},{4,2},{5,29},{6,4},{7,31},{8,14},{9,1},{... | collective-permute-start | bytes 3145736 | tf_op jit(solution)/shard_map/ppermute | solution.py:254
  47.3 4.4 %windows.1 = bf16[4,3,512,128]{3,2,1,0:T(8,128)(2,1)} custom-call(s32[5]{0:T(128)} %pad_add_fusion.s, f32[1024,128]{1,0:T(8,128)} %bitcast.63, f32[1024,128]{1,0:T(8,128)} %bitcast.64, f32[1024,128]{1,0:T(8,128)} %bitcast.65), custom_call_target="tpu_custom_call" | custom-call | flops 10000000 | bytes 4000000 | tf_op jit(solution)/shard_map/windows/pallas_call | solution.py:224
  51.7 5.3 %all-to-all-start = ((bf16[4,3,512,128]{3,2,1,0:T(8,128)(2,1)}), bf16[4,3,512,128]{3,2,1,0:T(8,128)(2,1)S(1)}, u32[]{:S(2)}, u32[]{:S(2)}) async-start(bf16[4,3,512,128]{3,2,1,0:T(8,128)(2,1)} %windows.1), calls=%async_computation | async-start | bytes 3145728 | tf_op jit(solution)/shard_map/all_to_all | solution.py:257
  57.0 11.3 %chip_product.3 = (f32[256,2048]{1,0:T(8,128)}, bf16[256,2048]{1,0:T(8,128)(2,1)}, bf16[256,2048]{1,0:T(8,128)(2,1)}, bf16[256,2048]{1,0:T(8,128)(2,1)}) custom-call(bf16[1536,1024]{1,0:T(8,128)(2,1)} %get-tuple-element.49.c, bf16[1536,4096]{1,0:T(8,128)(2,1)} %g.7, bf16[1024,2048]{1,0:T(8,128)(2,1)} %collective-permute-done.4.r), custom_call_target="tpu_custom_call" | custom-call | flops 402653184 | bytes 655360 | tf_op jit(solution)/shard_map/chip_product/pallas_call | solution.py:182
  68.3 2.7 %collective-permute-start.6 = (bf16[256,2048]{1,0:T(8,128)(2,1)}, bf16[256,2048]{1,0:T(8,128)(2,1)}, u32[]{:S(2)}, u32[]{:S(2)}) collective-permute-start(bf16[256,2048]{1,0:T(8,128)(2,1)} %get-tuple-element.56), channel_id=1, source_target_pairs={{0,4},{1,17},{2,6},{3,19},{4,0},{5,21},{6,2},{7,23},{8,12},{9,25},... | collective-permute-start | bytes 3145736 | tf_op jit(solution)/shard_map/ppermute | solution.py:260
  71.0 3.8 %add_convert_fusion.1 = bf16[256,2048]{1,0:T(8,128)(2,1)} fusion(bf16[256,2048]{1,0:T(8,128)(2,1)} %collective-permute-done.3, bf16[256,2048]{1,0:T(8,128)(2,1)} %collective-permute-done.2, f32[256,2048]{1,0:T(8,128)} %get-tuple-element.45, bf16[256,2048]{1,0:T(8,128)(2,1)S(1)} %collective-permute-done.1), kind=kLoop, calls=%fused_computation.4 | loop fusion | flops 3670016 | bytes 6291456 | tf_op jit(solution)/shard_map/convert_element_type | solution.py:269
  74.8 2.4 %all-to-all-done = bf16[4,3,512,128]{3,2,1,0:T(8,128)(2,1)S(1)} async-done(((bf16[4,3,512,128]{3,2,1,0:T(8,128)(2,1)}), bf16[4,3,512,128]{3,2,1,0:T(8,128)(2,1)S(1)}, u32[]{:S(2)}, u32[]{:S(2)}) %all-to-all-start) | async-done | bytes 1572896 | tf_op jit(solution)/shard_map/all_to_all | solution.py:257
  77.2 5.1 %all-to-all-start.1 = ((bf16[16,16,2048]{2,1,0:T(8,128)(2,1)}), bf16[16,16,2048]{2,1,0:T(8,128)(2,1)S(1)}, u32[]{:S(2)}, u32[]{:S(2)}) async-start(bf16[16,16,2048]{2,1,0:T(8,128)(2,1)} %bitcast.60), calls=%async_computation.1 | async-start | bytes 2097152 | tf_op jit(solution)/shard_map/all_to_all | solution.py:270
  82.4 1.1 collective-permute-done.7
  83.4 2.0 %collective-permute-done.6 = bf16[256,2048]{1,0:T(8,128)(2,1)} collective-permute-done((bf16[256,2048]{1,0:T(8,128)(2,1)}, bf16[256,2048]{1,0:T(8,128)(2,1)}, u32[]{:S(2)}, u32[]{:S(2)}) %collective-permute-start.6) | collective-permute-done | bytes 1048608 | tf_op jit(solution)/shard_map/ppermute | solution.py:260
  85.5 16.4 %collective-permute-done.5 = bf16[256,2048]{1,0:T(8,128)(2,1)} collective-permute-done((bf16[256,2048]{1,0:T(8,128)(2,1)}, bf16[256,2048]{1,0:T(8,128)(2,1)}, u32[]{:S(2)}, u32[]{:S(2)}) %collective-permute-start.5) | collective-permute-done | bytes 1048608 | tf_op jit(solution)/shard_map/ppermute | solution.py:260
  101.9 4.1 %add_convert_fusion = bf16[256,2048]{1,0:T(8,128)(2,1)} fusion(bf16[256,2048]{1,0:T(8,128)(2,1)} %collective-permute-done.7, bf16[256,2048]{1,0:T(8,128)(2,1)} %collective-permute-done.6, f32[256,2048]{1,0:T(8,128)} %get-tuple-element.54, bf16[256,2048]{1,0:T(8,128)(2,1)} %collective-permute-done.5), kind=kLoop, calls=%fused_computation.2 | loop fusion | flops 3670016 | bytes 6291456 | tf_op jit(solution)/shard_map/convert_element_type | solution.py:269
  106.0 7.6 %all-to-all-start.2 = ((bf16[16,16,2048]{2,1,0:T(8,128)(2,1)}), bf16[16,16,2048]{2,1,0:T(8,128)(2,1)}, u32[]{:S(2)}, u32[]{:S(2)}) async-start(bf16[16,16,2048]{2,1,0:T(8,128)(2,1)} %bitcast.61), calls=%async_computation.2 | async-start | bytes 2097152 | tf_op jit(solution)/shard_map/all_to_all | solution.py:270
  114.2 13.1 %all-to-all-done.2 = bf16[16,16,2048]{2,1,0:T(8,128)(2,1)} async-done(((bf16[16,16,2048]{2,1,0:T(8,128)(2,1)}), bf16[16,16,2048]{2,1,0:T(8,128)(2,1)}, u32[]{:S(2)}, u32[]{:S(2)}) %all-to-all-start.2) | async-done | bytes 1048608 | tf_op jit(solution)/shard_map/all_to_all | solution.py:270
  127.3 1.4 convert_reduce_fusion.1
  129.1 0.8 broadcast_in_dim.22
  129.9 3.5 %all-to-all-start.3 = ((bf16[4,16,4096]{2,1,0:T(8,128)(2,1)}), bf16[4,16,4096]{2,1,0:T(8,128)(2,1)S(1)}, u32[]{:S(2)}, u32[]{:S(2)}) async-start(bf16[4,16,4096]{2,1,0:T(8,128)(2,1)} %broadcast_in_dim.22), calls=%async_computation.3 | async-start | bytes 1048576 | tf_op jit(solution)/shard_map/all_to_all | solution.py:279
  135.6 5.9 %all-to-all-done.3 = bf16[4,16,4096]{2,1,0:T(8,128)(2,1)S(1)} async-done(((bf16[4,16,4096]{2,1,0:T(8,128)(2,1)}), bf16[4,16,4096]{2,1,0:T(8,128)(2,1)S(1)}, u32[]{:S(2)}, u32[]{:S(2)}) %all-to-all-start.3) | async-done | bytes 524320 | tf_op jit(solution)/shard_map/all_to_all | solution.py:279
  141.4 0.8 copy.11
  (24 shorter events, 4.8 us)
Async XLA Ops:
  18.1 11.4 %collective-permute-start = (bf16[1024,2048]{1,0:T(8,128)(2,1)}, bf16[1024,2048]{1,0:T(8,128)(2,1)}, u32[]{:S(2)}, u32[]{:S(2)}) collective-permute-start(bf16[1024,2048]{1,0:T(8,128)(2,1)} %get-tuple-element.31), channel_id=1, source_target_pairs={{0,1},{1,0},{2,3},{3,2},{4,5},{5,4},{6,7},{7,6},{8,9},{9,8},{10,11... | collective-permute-start | bytes 12582920 | tf_op jit(solution)/shard_map/ppermute | solution.py:248
  29.0 28.0 %collective-permute-start.4 = (bf16[1024,2048]{1,0:T(8,128)(2,1)}, bf16[1024,2048]{1,0:T(8,128)(2,1)}, u32[]{:S(2)}, u32[]{:S(2)}) collective-permute-start(bf16[1024,2048]{1,0:T(8,128)(2,1)} %other_product.1), channel_id=1, source_target_pairs={{0,1},{1,0},{2,3},{3,2},{4,5},{5,4},{6,7},{7,6},{8,9},{9,8},{10,11... | collective-permute-start | bytes 12582920 | tf_op jit(solution)/shard_map/ppermute | solution.py:250
  29.5 17.2 %copy-start = (s32[1,4]{1,0:T(1,128)S(1)}, s32[1,4]{1,0:T(1,128)}, u32[]{:S(2)}) copy-start(s32[1,4]{1,0:T(1,128)} %param.11) | copy-start | bytes 52
  40.8 30.2 %collective-permute-start.1 = (bf16[256,2048]{1,0:T(8,128)(2,1)}, bf16[256,2048]{1,0:T(8,128)(2,1)S(1)}, u32[]{:S(2)}, u32[]{:S(2)}) collective-permute-start(bf16[256,2048]{1,0:T(8,128)(2,1)} %get-tuple-element.46), channel_id=1, source_target_pairs={{0,2},{1,9},{2,4},{3,11},{4,6},{5,13},{6,0},{7,15},{8,10},{9,17},{... | collective-permute-start | bytes 3145736 | tf_op jit(solution)/shard_map/ppermute | solution.py:254
  42.5 28.5 %collective-permute-start.2 = (bf16[256,2048]{1,0:T(8,128)(2,1)}, bf16[256,2048]{1,0:T(8,128)(2,1)}, u32[]{:S(2)}, u32[]{:S(2)}) collective-permute-start(bf16[256,2048]{1,0:T(8,128)(2,1)} %get-tuple-element.47), channel_id=1, source_target_pairs={{0,4},{1,17},{2,6},{3,19},{4,0},{5,21},{6,2},{7,23},{8,12},{9,25},... | collective-permute-start | bytes 3145736 | tf_op jit(solution)/shard_map/ppermute | solution.py:254
  45.2 25.8 %collective-permute-start.3 = (bf16[256,2048]{1,0:T(8,128)(2,1)}, bf16[256,2048]{1,0:T(8,128)(2,1)}, u32[]{:S(2)}, u32[]{:S(2)}) collective-permute-start(bf16[256,2048]{1,0:T(8,128)(2,1)} %get-tuple-element.48), channel_id=1, source_target_pairs={{0,6},{1,25},{2,0},{3,27},{4,2},{5,29},{6,4},{7,31},{8,14},{9,1},{... | collective-permute-start | bytes 3145736 | tf_op jit(solution)/shard_map/ppermute | solution.py:254
  51.7 25.6 %all-to-all-start = ((bf16[4,3,512,128]{3,2,1,0:T(8,128)(2,1)}), bf16[4,3,512,128]{3,2,1,0:T(8,128)(2,1)S(1)}, u32[]{:S(2)}, u32[]{:S(2)}) async-start(bf16[4,3,512,128]{3,2,1,0:T(8,128)(2,1)} %windows.1), calls=%async_computation | async-start | bytes 3145728 | tf_op jit(solution)/shard_map/all_to_all | solution.py:257
  68.3 15.1 %collective-permute-start.7 = (bf16[256,2048]{1,0:T(8,128)(2,1)}, bf16[256,2048]{1,0:T(8,128)(2,1)}, u32[]{:S(2)}, u32[]{:S(2)}) collective-permute-start(bf16[256,2048]{1,0:T(8,128)(2,1)} %get-tuple-element.57), channel_id=1, source_target_pairs={{0,6},{1,25},{2,0},{3,27},{4,2},{5,29},{6,4},{7,31},{8,14},{9,1},{... | collective-permute-start | bytes 3145736 | tf_op jit(solution)/shard_map/ppermute | solution.py:260
  68.3 17.1 %collective-permute-start.6 = (bf16[256,2048]{1,0:T(8,128)(2,1)}, bf16[256,2048]{1,0:T(8,128)(2,1)}, u32[]{:S(2)}, u32[]{:S(2)}) collective-permute-start(bf16[256,2048]{1,0:T(8,128)(2,1)} %get-tuple-element.56), channel_id=1, source_target_pairs={{0,4},{1,17},{2,6},{3,19},{4,0},{5,21},{6,2},{7,23},{8,12},{9,25},... | collective-permute-start | bytes 3145736 | tf_op jit(solution)/shard_map/ppermute | solution.py:260
  71.0 30.9 %collective-permute-start.5 = (bf16[256,2048]{1,0:T(8,128)(2,1)}, bf16[256,2048]{1,0:T(8,128)(2,1)}, u32[]{:S(2)}, u32[]{:S(2)}) collective-permute-start(bf16[256,2048]{1,0:T(8,128)(2,1)} %get-tuple-element.55), channel_id=1, source_target_pairs={{0,2},{1,9},{2,4},{3,11},{4,6},{5,13},{6,0},{7,15},{8,10},{9,17},{... | collective-permute-start | bytes 3145736 | tf_op jit(solution)/shard_map/ppermute | solution.py:260
  77.2 28.8 %all-to-all-start.1 = ((bf16[16,16,2048]{2,1,0:T(8,128)(2,1)}), bf16[16,16,2048]{2,1,0:T(8,128)(2,1)S(1)}, u32[]{:S(2)}, u32[]{:S(2)}) async-start(bf16[16,16,2048]{2,1,0:T(8,128)(2,1)} %bitcast.60), calls=%async_computation.1 | async-start | bytes 2097152 | tf_op jit(solution)/shard_map/all_to_all | solution.py:270
  106.0 21.3 %all-to-all-start.2 = ((bf16[16,16,2048]{2,1,0:T(8,128)(2,1)}), bf16[16,16,2048]{2,1,0:T(8,128)(2,1)}, u32[]{:S(2)}, u32[]{:S(2)}) async-start(bf16[16,16,2048]{2,1,0:T(8,128)(2,1)} %bitcast.61), calls=%async_computation.2 | async-start | bytes 2097152 | tf_op jit(solution)/shard_map/all_to_all | solution.py:270
  129.9 11.5 %all-to-all-start.3 = ((bf16[4,16,4096]{2,1,0:T(8,128)(2,1)}), bf16[4,16,4096]{2,1,0:T(8,128)(2,1)S(1)}, u32[]{:S(2)}, u32[]{:S(2)}) async-start(bf16[4,16,4096]{2,1,0:T(8,128)(2,1)} %broadcast_in_dim.22), calls=%async_computation.3 | async-start | bytes 1048576 | tf_op jit(solution)/shard_map/all_to_all | solution.py:279

commit v3 on v2

v3 whole, which is shorter than its diff:
```python
import jax
import jax.numpy as jnp
from jax import lax
from jax.experimental import pallas as pl
from jax.experimental.pallas import tpu as pltpu
from jax.sharding import PartitionSpec as P

beta_one = 0.9
beta_two = 0.95
step_size = 0.01
epsilon = 1e-08

N_GRP = 4
ROWS = 64
CHUNKS = (2048, 2048)
TILE = 512
f32, bf16 = jnp.float32, jnp.bfloat16
AXES = ("grp", "shard")

DEVICES = [(z, y, x, c) for z in range(4) for y in range(4) for x in range(4) for c in range(2)]
SWAP = [(i, i ^ 1) for i in range(128)]


def number(z, y, x, c):
    return (((z % 4) * 4 + y % 4) * 4 + x % 4) * 2 + c


FIRST = {
    k: [(number(z, y, x, c), number(z, y + k * c, x + k * (1 - c), c)) for z, y, x, c in DEVICES] for k in (1, 2, 3)
}


def grouped(key, order):
    groups = {}
    for place in sorted(DEVICES, key=lambda place: order(*place)):
        groups.setdefault(key(*place), []).append(number(*place))
    return list(groups.values())


THIRD = {k: [(number(z, y, x, c), number(z + k, y, x, c)) for z, y, x, c in DEVICES] for k in (1, 2, 3)}
ALONG_FIRST = grouped(lambda z, y, x, c: (z, c, x if c else y), lambda z, y, x, c: (y, x))
SECOND = grouped(lambda z, y, x, c: (c, y if c else x), lambda z, y, x, c: (y, x, z))


def row_block(shard, core, i):
    x, y, j1, d2 = (shard >> 1) & 3, shard >> 3, i // 4, i % 4
    return jnp.where(core == 0, d2 * 4 + ((x + j1) & 3), ((y + j1) & 3) * 4 + d2)


def params():
    return pltpu.CompilerParams(vmem_limit_bytes=60 * 2**20)


def cost(tokens, height, cols):
    return pl.CostEstimate(
        flops=2 * tokens * height * cols // 16, bytes_accessed=(tokens + height) * cols // 8, transcendentals=0
    )


def product(left, right):
    return lax.dot_general(left, right, (((0,), (0,)), ((), ())), preferred_element_type=f32)


def first_product(shard, context, out_grad, start, cols):
    tokens, height = context.shape
    half, parts = height // 2, 4
    slab = tokens // parts

    def body(t, c_hbm, g, out, mine_hbm, other_hbm, c, mine, other, arrived, left):
        step = pl.program_id(0)

        def piece(m):
            at = pl.ds(m * slab, slab)
            return pltpu.make_async_copy(c_hbm.at[at], c.at[at], arrived.at[m])

        def away():
            return [
                pltpu.make_async_copy(mine, mine_hbm, left.at[0]),
                pltpu.make_async_copy(other, other_hbm, left.at[1]),
            ]

        def choose(to, core):
            for m in range(parts):
                at = pl.ds(m * slab, slab)
                for k in range(8):
                    low, high = [
                        c[at, pl.ds(pl.multiple_of(row_block(t[0], core, 2 * k + i) * 128, 128), 128)] for i in (0, 1)
                    ]
                    to[at, pl.ds(k * 128, 128)] = jnp.concatenate(
                        [low[:, core * 64:core * 64 + 64], high[:, core * 64:core * 64 + 64]], axis=1
                    )

        @pl.when(step == 0)
        def _():
            for m in range(parts):
                piece(m).start()
            for m in range(parts):
                piece(m).wait()

            @pl.when((t[0] & 1) == 0)
            def _():
                choose(other, 1)
                choose(mine, 0)

            @pl.when((t[0] & 1) == 1)
            def _():
                choose(other, 0)
                choose(mine, 1)

            for copy in away():
                copy.start()

        out[...] = product(other[...], g[...]).astype(bf16)

        @pl.when(step == cols // TILE - 1)
        def _():
            for copy in away():
                copy.wait()

    hbm = pl.BlockSpec(memory_space=pl.ANY)
    return pl.pallas_call(
        body,
        grid_spec=pltpu.PrefetchScalarGridSpec(
            num_scalar_prefetch=1,
            grid=(cols // TILE,),
            in_specs=[hbm, pl.BlockSpec((tokens, TILE), lambda i, t: (0, start // TILE + i))],
            out_specs=[pl.BlockSpec((half, TILE), lambda i, t: (0, i)), hbm, hbm],
            scratch_shapes=[
                pltpu.VMEM((tokens, height), bf16),
                pltpu.VMEM((tokens, half), bf16),
                pltpu.VMEM((tokens, half), bf16),
                pltpu.SemaphoreType.DMA((parts,)),
                pltpu.SemaphoreType.DMA((2,)),
            ],
        ),
        out_shape=[
            jax.ShapeDtypeStruct((half, cols), bf16),
            jax.ShapeDtypeStruct((tokens, half), bf16),
            jax.ShapeDtypeStruct((tokens, half), bf16),
        ],
        name="first_product",
        cost_estimate=cost(tokens, half, cols),
        compiler_params=params(),
    )(shard, context, out_grad)


def other_product(other, out_grad, start, cols):
    tokens, half = other.shape

    def body(c, g, out):
        out[...] = product(c[...], g[...]).astype(bf16)

    return pl.pallas_call(
        body,
        grid=(cols // TILE,),
        in_specs=[
            pl.BlockSpec((tokens, half), lambda i: (0, 0), pipeline_mode=pl.Buffered(1)),
            pl.BlockSpec((tokens, TILE), lambda i: (0, start // TILE + i)),
        ],
        out_specs=pl.BlockSpec((half, TILE), lambda i: (0, i)),
        out_shape=jax.ShapeDtypeStruct((half, cols), bf16),
        name="other_product",
        cost_estimate=cost(tokens, half, cols),
        compiler_params=params(),
    )(other, out_grad)


def chip_product(shard, mine, out_grad, received, start, cols, by_place):
    tokens, half = mine.shape
    quarter = half // 4

    def body(t, c, g, r, own, *away):
        total = product(c[...], g[...]) + r[...].astype(f32)
        own[...] = total[:quarter]
        if by_place:
            place = jnp.where((t[0] & 1) == 0, (t[0] >> 1) & 3, t[0] >> 3)
            for k in range(4):
                away[0][(place + k) & 3] = total[k * quarter:(k + 1) * quarter].astype(bf16)
        else:
            for k in range(3):
                away[k][...] = total[(k + 1) * quarter:(k + 2) * quarter].astype(bf16)

    spec = pl.BlockSpec((quarter, TILE), lambda i, t: (0, i))
    if by_place:
        specs, shapes = [pl.BlockSpec((4, quarter, TILE), lambda i, t: (0, 0, i))], [(4, quarter, cols)]
    else:
        specs, shapes = [spec] * 3, [(quarter, cols)] * 3
    return pl.pallas_call(
        body,
        grid_spec=pltpu.PrefetchScalarGridSpec(
            num_scalar_prefetch=1,
            grid=(cols // TILE,),
            in_specs=[
                pl.BlockSpec((tokens, half), lambda i, t: (0, 0), pipeline_mode=pl.Buffered(1)),
                pl.BlockSpec((tokens, TILE), lambda i, t: (0, start // TILE + i)),
                pl.BlockSpec((half, TILE), lambda i, t: (0, i)),
            ],
            out_specs=[spec] + specs,
        ),
        out_shape=[jax.ShapeDtypeStruct((quarter, cols), f32)] + [jax.ShapeDtypeStruct(shape, bf16) for shape in shapes],
        name="chip_product",
        cost_estimate=cost(tokens, half, cols),
        compiler_params=params(),
    )(shard, mine, out_grad, received)


def windows(lengths, group, pieces):
    cap = pieces[0].size
    n, rows = cap // 256, cap // 128

    def body(s, g, p0, p1, p2, *refs):
        group, held = g[0], refs[N_GRP]
        begin = jnp.int32(0)
        for k in range(N_GRP):
            begin = begin + jnp.where(k < group, s[k], 0)
        length = s[group]
        lane = lax.broadcasted_iota(jnp.int32, (n, 128), 1)
        at = lax.broadcasted_iota(jnp.int32, (n, 128), 0) * 128 + lane
        for k, piece in enumerate((p0, p1, p2)):
            held[pl.ds(n, rows), :] = piece[...]
            for further in range(N_GRP):
                offset = ((group + further) & (N_GRP - 1)) * (n * 128) - begin
                first = jnp.clip(offset >> 7, -n, rows) + n
                turn = offset & 127
                back = (128 - turn) & 127
                low = pltpu.roll(held[pl.ds(first, n), :], back, 1)
                high = pltpu.roll(held[pl.ds(first + 1, n), :], back, 1)
                value = jnp.where(lane < 128 - turn, low, high)
                inside = (at + offset >= 0) & (at + offset < length)
                refs[further][k] = jnp.where(inside, value, 0.0).astype(bf16)

    whole = pl.BlockSpec((rows, 128), lambda i, s, g: (0, 0))
    return pl.pallas_call(
        body,
        grid_spec=pltpu.PrefetchScalarGridSpec(
            num_scalar_prefetch=2,
            grid=(1,),
            in_specs=[whole] * 3,
            out_specs=[pl.BlockSpec((3, n, 128), lambda i, s, g: (0, 0, 0))] * N_GRP,
            scratch_shapes=[pltpu.VMEM((rows + 2 * n + 8, 128), f32)],
        ),
        out_shape=[jax.ShapeDtypeStruct((3, n, 128), bf16)] * N_GRP,
        name="windows",
        cost_estimate=pl.CostEstimate(flops=10**7, bytes_accessed=4 * 10**6, transcendentals=0),
        compiler_params=params(),
    )(lengths, group, *[a.reshape(rows, 128) for a in pieces])


def local(context, out_grad, old_master, old_mom1, old_mom2, old_lengths):
    width = out_grad.shape[1]
    shard, group = lax.axis_index("shard")[None], lax.axis_index("grp")[None]
    first_cols, second_cols = CHUNKS

    theirs, mine, other = first_product(shard, context, out_grad, 0, first_cols)
    received = lax.ppermute(theirs, AXES, SWAP)
    theirs = other_product(other, out_grad, first_cols, second_cols)
    received_later = lax.ppermute(theirs, AXES, SWAP)
    (received, mine), theirs = lax.optimization_barrier(((received, mine), theirs))
    own, away = chip_product(shard, mine, out_grad, received, 0, first_cols, True)
    (own, away), mine = lax.optimization_barrier(((own, away), mine))
    arrived = lax.all_to_all(away, AXES, 0, 0, axis_index_groups=ALONG_FIRST, tiled=True)
    own_later, *away = chip_product(shard, mine, out_grad, received_later, first_cols, second_cols, False)
    pieces = (old_master, old_mom1, old_mom2)
    pieces, own_later = lax.optimization_barrier((pieces, own_later))
    arrived_later = [lax.ppermute(away[k - 1], AXES, FIRST[k]) for k in (1, 2, 3)]
    keep, *cut = windows(old_lengths[0], group, pieces)
    (keep, cut), own = lax.optimization_barrier(((keep, cut), own))
    cut = [lax.ppermute(cut[k - 1], AXES, THIRD[k]) for k in (1, 2, 3)]
    state = sum([value.astype(f32) for value in cut], keep.astype(f32)).reshape(3, ROWS // N_GRP, width)

    def first_sum(own, arrived):
        return sum([value.astype(f32) for value in arrived], own).astype(bf16)

    def owners(summed):
        summed = summed.reshape(16, ROWS // N_GRP, -1)
        return lax.all_to_all(summed, AXES, 0, 0, axis_index_groups=SECOND, tiled=True)

    def step(state, gradient):
        gradient = jnp.sum(gradient.astype(f32), axis=0)
        master, first, second = state
        first_new = beta_one * first + (1.0 - beta_one) * gradient
        second_new = beta_two * second + (1.0 - beta_two) * gradient * gradient
        return master - step_size * first_new / (jnp.sqrt(second_new) + epsilon), first_new, second_new

    place = jnp.where(shard[0] % 2 == 0, shard[0] // 2 % 4, shard[0] // 8)
    summed = first_sum(own, [jnp.where(place == k, 0.0, arrived[k].astype(f32)) for k in range(4)])
    summed, own_later = lax.optimization_barrier((summed, own_later))
    own_later, state = lax.optimization_barrier((own_later, state))
    terms = owners(summed)
    summed_later = first_sum(own_later, arrived_later)
    summed_later, terms = lax.optimization_barrier((summed_later, terms))
    terms_later = owners(summed_later)
    def to_groups(part):
        parts = [part] + [lax.ppermute(part, AXES, THIRD[k]) for k in (1, 2, 3)]
        whole = jnp.zeros((N_GRP,) + part.shape, bf16)
        for k, part in enumerate(parts):
            whole = lax.dynamic_update_index_in_dim(whole, part, (group[0] - k) % N_GRP, 0)
        return whole.reshape(ROWS, -1)

    result = step(state[:, :, :first_cols], terms)
    weights = to_groups(result[0].astype(bf16))
    weights, terms_later = lax.optimization_barrier((weights, terms_later))
    result_later = step(state[:, :, first_cols:], terms_later)
    weights = [weights, to_groups(result_later[0].astype(bf16))]
    outputs = [*zip(result, result_later), weights]
    return tuple(jnp.concatenate(parts, axis=1)[None] for parts in outputs)


def solution(mesh):
    placed = (
        P(("grp", "shard"), None),
        P(("grp", "shard"), None),
        P("shard", "grp", None),
        P("shard", "grp", None),
        P("shard", "grp", None),
        P("shard", None),
    )
    return jax.shard_map(
        local,
        mesh=mesh,
        in_specs=placed,
        out_specs=(
            P("shard", "grp", None),
            P("shard", "grp", None),
            P("shard", "grp", None),
            P("shard", None, None),
        ),
        check_vma=False,
    )
```

time: 143 us -> 138 us (0.965)
  waiting for transfers between devices: 40.9 us -> 23.9 us
  starting transfers between devices: 30.6 us -> 46.1 us
  local copies, waits for them, and re-layouts: 1.77 us -> 0.25 us
    ppermute x3, waiting for transfers between devices: 19.5 us -> 6.15 us  [local(): lax.ppermute(away[k - 1], AXES, FIRST[k])]
    ppermute x3 -> x9, starting transfers between devices: 5.83 us -> 17.5 us  [the longest x6 9.3 us: to_groups(): parts = [part] + [lax.ppermute(part, AXES, THIRD[k]) for k in (1, 2, 3)]]
    all_to_all x4 -> x3, waiting for transfers between devices: 21.4 us -> 14 us  [the longest x2 14 us: owners(): lax.all_to_all(summed, AXES, 0, 0, axis_index_groups=SECOND, tiled=True)]
    ppermute x3 -> x9, waiting for transfers between devices: 0.01 us -> 3.73 us  [the longest x3 2.18 us: local(): cut = [lax.ppermute(cut[k - 1], AXES, THIRD[k]) for k in (1, 2, 3)]]
    ppermute x3, starting transfers between devices: 2.67 us -> 5.9 us  [local(): lax.ppermute(away[k - 1], AXES, FIRST[k])]
    reduce_sum x3 -> x2, other arithmetic: 1.75 us -> 0.3 us  [step(): gradient = jnp.sum(gradient.astype(f32), axis=0)]
    all_to_all x4 -> x3, starting transfers between devices: 21.5 us -> 22.1 us  [the longest x2 17.1 us: owners(): lax.all_to_all(summed, AXES, 0, 0, axis_index_groups=SECOND, tiled=True)]
    convert_element_type x2 -> x4, other arithmetic: 7.96 us -> 8.45 us  [the longest x2 8.25 us: first_sum(): return sum([value.astype(f32) for value in arrived], own).astype(bf16)]
  transfers between devices with their start and end apart: 12 -> 17, of which waited for: 6 -> 6; matrix products, arithmetic and copies ran while one was open for 8% -> 8% of each run, Pallas kernels for 27% -> 27%
where the time goes in v3:
time: 138 us
  Pallas kernels  54 us (39%)
  starting transfers between devices  46.1 us (33%)
  waiting for transfers between devices  23.9 us (17%)
  other arithmetic  12.5 us (9%)
    pallas_call x2, Pallas kernels, chip_product(): pl.pallas_call(body, grid_spec=pltpu.PrefetchScalarGridSpec(num_scalar_pr...  22.9 us
    all_to_all x2, starting transfers between devices, owners(): lax.all_to_all(summed, AXES, 0, 0, axis_index_groups=SECOND, tiled=True)  17.1 us
    pallas_call x1, Pallas kernels, first_product(): pl.pallas_call(body, grid_spec=pltpu.PrefetchScalarGridSpec(num_scalar_pr...  16.2 us
    all_to_all x2, waiting for transfers between devices, owners(): lax.all_to_all(summed, AXES, 0, 0, axis_index_groups=SECOND, tiled=True)  14 us
    pallas_call x1, Pallas kernels, other_product(): pl.pallas_call(body, grid=(cols // TILE,), in_specs=[pl.BlockSpec((tokens...  10.8 us
    ppermute x6, starting transfers between devices, to_groups(): parts = [part] + [lax.ppermute(part, AXES, THIRD[k]) for k in (1, 2, 3)]  9.3 us
    convert_element_type x2, other arithmetic, first_sum(): return sum([value.astype(f32) for value in arrived], own).astype(bf16)  8.25 us
    ppermute x3, starting transfers between devices, local(): cut = [lax.ppermute(cut[k - 1], AXES, THIRD[k]) for k in (1, 2, 3)]  8.25 us
  transfers between devices with their start and end apart: 17, of which 6 were waited for; matrix products, arithmetic and copies ran while one was open for 8% of the time, Pallas kernels for 27%

profile of v3, /device:TPU:0, one launch (start us, length us, event | category | flops | bytes accessed | tf_op | source)
XLA Modules:
  0.0 137.7 jit_solution(5089690523969122297)
XLA Ops:
  0.6 16.2 %first_product.1 = (bf16[1024,2048]{1,0:T(8,128)(2,1)}, bf16[1536,1024]{1,0:T(8,128)(2,1)}, bf16[1536,1024]{1,0:T(8,128)(2,1)}) custom-call(s32[1]{0:T(128)} %bitcast.2.t, bf16[1536,2048]{1,0:T(8,128)(2,1)} %c_hbm.1, bf16[1536,4096]{1,0:T(8,128)(2,1)} %g.7), custom_call_target="tpu_custom_call" | custom-call | flops 402653184 | bytes 655360 | tf_op jit(solution)/shard_map/first_product/pallas_call | solution.py:121
  16.9 10.8 %other_product.1 = bf16[1024,2048]{1,0:T(8,128)(2,1)} custom-call(bf16[1536,1024]{1,0:T(8,128)(2,1)} %get-tuple-element.41.c, bf16[1536,4096]{1,0:T(8,128)(2,1)} %g.7), custom_call_target="tpu_custom_call" | custom-call | flops 402653184 | bytes 655360 | tf_op jit(solution)/shard_map/other_product/pallas_call | solution.py:153
  28.2 11.4 %chip_product.2 = (f32[256,2048]{1,0:T(8,128)}, bf16[4,256,2048]{2,1,0:T(8,128)(2,1)}) custom-call(s32[1]{0:T(128)} %bitcast.2.t, bf16[1536,1024]{1,0:T(8,128)(2,1)} %get-tuple-element.46.c, bf16[1536,4096]{1,0:T(8,128)(2,1)} %g.7, bf16[1024,2048]{1,0:T(8,128)(2,1)} %collective-permute-done.r), custom_call_target="tpu_custom_call" | custom-call | flops 402653184 | bytes 655360 | tf_op jit(solution)/shard_map/chip_product/pallas_call | solution.py:188
  39.6 5.0 %all-to-all-start = ((bf16[4,256,2048]{2,1,0:T(8,128)(2,1)}), bf16[4,256,2048]{2,1,0:T(8,128)(2,1)}, u32[]{:S(2)}, u32[]{:S(2)}) async-start(bf16[4,256,2048]{2,1,0:T(8,128)(2,1)} %get-tuple-element.57), calls=%async_computation | async-start | bytes 8388608 | tf_op jit(solution)/shard_map/all_to_all | solution.py:261
  44.7 11.5 %chip_product.3 = (f32[256,2048]{1,0:T(8,128)}, bf16[256,2048]{1,0:T(8,128)(2,1)}, bf16[256,2048]{1,0:T(8,128)(2,1)}, bf16[256,2048]{1,0:T(8,128)(2,1)}) custom-call(s32[1]{0:T(128)} %bitcast.2.t, bf16[1536,1024]{1,0:T(8,128)(2,1)} %get-tuple-element.46.c, bf16[1536,4096]{1,0:T(8,128)(2,1)} %g.7, bf16[1024,2048]{1,0:T(8,128)(2,1)} %collective-permute-done.1.r), custom_call_target="tpu_custom_call" | custom-call | flops 402653184 | bytes 655360 | tf_op jit(solution)/shard_map/chip_product/pallas_call | solution.py:188
  56.1 4.2 %windows.1 = (bf16[3,512,128]{2,1,0:T(8,128)(2,1)}, bf16[3,512,128]{2,1,0:T(8,128)(2,1)}, bf16[3,512,128]{2,1,0:T(8,128)(2,1)}, bf16[3,512,128]{2,1,0:T(8,128)(2,1)}) custom-call(s32[4]{0:T(128)} %bitcast.95, s32[1]{0:T(128)} %bitcast.1.g, f32[1024,128]{1,0:T(8,128)} %bitcast.92, f32[1024,128]{1,0:T(8,128)} %bitcast.93, f32[1024,128]{1,0:T(8,128)} %bitcast.94), custom_call_target="tpu_custom_call" | custom-call | flops 10000000 | bytes 4000000 | tf_op jit(solution)/shard_map/windows/pallas_call | solution.py:233
  60.3 2.1 %collective-permute-start.2 = (bf16[3,512,128]{2,1,0:T(8,128)(2,1)}, bf16[3,512,128]{2,1,0:T(8,128)(2,1)S(1)}, u32[]{:S(2)}, u32[]{:S(2)}) collective-permute-start(bf16[3,512,128]{2,1,0:T(8,128)(2,1)} %get-tuple-element.61), channel_id=1, source_target_pairs={{0,32},{1,33},{2,34},{3,35},{4,36},{5,37},{6,38},{7,39},{8,40},{9,... | collective-permute-start | bytes 1179656 | tf_op jit(solution)/shard_map/ppermute | solution.py:268
  62.4 1.7 %collective-permute-start.5 = (bf16[256,2048]{1,0:T(8,128)(2,1)}, bf16[256,2048]{1,0:T(8,128)(2,1)}, u32[]{:S(2)}, u32[]{:S(2)}) collective-permute-start(bf16[256,2048]{1,0:T(8,128)(2,1)} %get-tuple-element.66), channel_id=1, source_target_pairs={{0,2},{1,9},{2,4},{3,11},{4,6},{5,13},{6,0},{7,15},{8,10},{9,17},{... | collective-permute-start | bytes 3145736 | tf_op jit(solution)/shard_map/ppermute | solution.py:265
  64.1 2.7 %collective-permute-start.6 = (bf16[256,2048]{1,0:T(8,128)(2,1)}, bf16[256,2048]{1,0:T(8,128)(2,1)}, u32[]{:S(2)}, u32[]{:S(2)}) collective-permute-start(bf16[256,2048]{1,0:T(8,128)(2,1)} %get-tuple-element.67), channel_id=1, source_target_pairs={{0,4},{1,17},{2,6},{3,19},{4,0},{5,21},{6,2},{7,23},{8,12},{9,25},... | collective-permute-start | bytes 3145736 | tf_op jit(solution)/shard_map/ppermute | solution.py:265
  66.8 1.5 %collective-permute-start.7 = (bf16[256,2048]{1,0:T(8,128)(2,1)}, bf16[256,2048]{1,0:T(8,128)(2,1)}, u32[]{:S(2)}, u32[]{:S(2)}) collective-permute-start(bf16[256,2048]{1,0:T(8,128)(2,1)} %get-tuple-element.68), channel_id=1, source_target_pairs={{0,6},{1,25},{2,0},{3,27},{4,2},{5,29},{6,4},{7,31},{8,14},{9,1},{... | collective-permute-start | bytes 3145736 | tf_op jit(solution)/shard_map/ppermute | solution.py:265
  68.3 3.5 %collective-permute-start.3 = (bf16[3,512,128]{2,1,0:T(8,128)(2,1)}, bf16[3,512,128]{2,1,0:T(8,128)(2,1)S(1)}, u32[]{:S(2)}, u32[]{:S(2)}) collective-permute-start(bf16[3,512,128]{2,1,0:T(8,128)(2,1)} %get-tuple-element.62), channel_id=1, source_target_pairs={{0,64},{1,65},{2,66},{3,67},{4,68},{5,69},{6,70},{7,71},{8,72},{9,... | collective-permute-start | bytes 1179656 | tf_op jit(solution)/shard_map/ppermute | solution.py:268
  71.8 2.2 %collective-permute-done.2 = bf16[3,512,128]{2,1,0:T(8,128)(2,1)S(1)} collective-permute-done((bf16[3,512,128]{2,1,0:T(8,128)(2,1)}, bf16[3,512,128]{2,1,0:T(8,128)(2,1)S(1)}, u32[]{:S(2)}, u32[]{:S(2)}) %collective-permute-start.2) | collective-permute-done | bytes 393248 | tf_op jit(solution)/shard_map/ppermute | solution.py:268
  74.0 2.7 %collective-permute-start.4 = (bf16[3,512,128]{2,1,0:T(8,128)(2,1)}, bf16[3,512,128]{2,1,0:T(8,128)(2,1)}, u32[]{:S(2)}, u32[]{:S(2)}) collective-permute-start(bf16[3,512,128]{2,1,0:T(8,128)(2,1)} %get-tuple-element.63), channel_id=1, source_target_pairs={{0,96},{1,97},{2,98},{3,99},{4,100},{5,101},{6,102},{7,103},{8,104... | collective-permute-start | bytes 1179656 | tf_op jit(solution)/shard_map/ppermute | solution.py:268
  76.6 4.1 %fusion = bf16[256,2048]{1,0:T(8,128)(2,1)} fusion(f32[256,2048]{1,0:T(8,128)S(1)} %copy-done, bf16[4,256,2048]{2,1,0:T(8,128)(2,1)} %all-to-all-done, pred[]{:T(512)S(6)} %eq.30, pred[]{:T(512)S(6)} %eq.29, pred[]{:T(512)S(6)} %eq.28, pred[]{:T(512)S(6)} %eq.27), kind=kLoop, calls=%fused_computation.1 | loop fusion | flops 6815744 | bytes 7340036 | tf_op jit(solution)/shard_map/convert_element_type | solution.py:272
  80.8 12.0 %all-to-all-start.1 = ((bf16[16,16,2048]{2,1,0:T(8,128)(2,1)}), bf16[16,16,2048]{2,1,0:T(8,128)(2,1)S(1)}, u32[]{:S(2)}, u32[]{:S(2)}) async-start(bf16[16,16,2048]{2,1,0:T(8,128)(2,1)} %bitcast.12), calls=%async_computation.1 | async-start | bytes 2097152 | tf_op jit(solution)/shard_map/all_to_all | solution.py:276
  92.9 1.2 convert_add_fusion
  94.3 6.1 %collective-permute-done.6 = bf16[256,2048]{1,0:T(8,128)(2,1)} collective-permute-done((bf16[256,2048]{1,0:T(8,128)(2,1)}, bf16[256,2048]{1,0:T(8,128)(2,1)}, u32[]{:S(2)}, u32[]{:S(2)}) %collective-permute-start.6) | collective-permute-done | bytes 1048608 | tf_op jit(solution)/shard_map/ppermute | solution.py:265
  100.4 4.1 %add_convert_fusion = bf16[256,2048]{1,0:T(8,128)(2,1)} fusion(bf16[256,2048]{1,0:T(8,128)(2,1)} %collective-permute-done.7, bf16[256,2048]{1,0:T(8,128)(2,1)} %collective-permute-done.6, f32[256,2048]{1,0:T(8,128)} %get-tuple-element.65, bf16[256,2048]{1,0:T(8,128)(2,1)} %collective-permute-done.5), kind=kLoop, calls=%fused_computation.7 | loop fusion | flops 3670016 | bytes 6291456 | tf_op jit(solution)/shard_map/convert_element_type | solution.py:272
  104.5 1.2 all-to-all-done.1
  106.9 3.6 %collective-permute-start.9 = (bf16[16,2048]{1,0:T(8,128)(2,1)S(1)}, bf16[16,2048]{1,0:T(8,128)(2,1)S(1)}, u32[]{:S(2)}, u32[]{:S(2)}) collective-permute-start(bf16[16,2048]{1,0:T(8,128)(2,1)S(1)} %get-tuple-element.78), channel_id=1, source_target_pairs={{0,64},{1,65},{2,66},{3,67},{4,68},{5,69},{6,70},{7,71},{8,72},{9,... | collective-permute-start | bytes 196616 | tf_op jit(solution)/shard_map/ppermute | solution.py:294
  111.5 5.0 %all-to-all-start.2 = ((bf16[16,16,2048]{2,1,0:T(8,128)(2,1)}), bf16[16,16,2048]{2,1,0:T(8,128)(2,1)S(1)}, u32[]{:S(2)}, u32[]{:S(2)}) async-start(bf16[16,16,2048]{2,1,0:T(8,128)(2,1)} %bitcast.21), calls=%async_computation.2 | async-start | bytes 2097152 | tf_op jit(solution)/shard_map/all_to_all | solution.py:276
  116.7 12.8 %all-to-all-done.2 = bf16[16,16,2048]{2,1,0:T(8,128)(2,1)S(1)} async-done(((bf16[16,16,2048]{2,1,0:T(8,128)(2,1)}), bf16[16,16,2048]{2,1,0:T(8,128)(2,1)S(1)}, u32[]{:S(2)}, u32[]{:S(2)}) %all-to-all-start.2) | async-done | bytes 1048608 | tf_op jit(solution)/shard_map/all_to_all | solution.py:276
  130.5 1.6 %collective-permute-start.12 = (bf16[16,2048]{1,0:T(8,128)(2,1)S(1)}, bf16[16,2048]{1,0:T(8,128)(2,1)S(1)}, u32[]{:S(2)}, u32[]{:S(2)}) collective-permute-start(bf16[16,2048]{1,0:T(8,128)(2,1)S(1)} %get-tuple-element.74), channel_id=1, source_target_pairs={{0,64},{1,65},{2,66},{3,67},{4,68},{5,69},{6,70},{7,71},{8,72},{9,... | collective-permute-start | bytes 196616 | tf_op jit(solution)/shard_map/ppermute | solution.py:294
  132.1 1.6 %collective-permute-start.13 = (bf16[16,2048]{1,0:T(8,128)(2,1)S(1)}, bf16[16,2048]{1,0:T(8,128)(2,1)S(1)}, u32[]{:S(2)}, u32[]{:S(2)}) collective-permute-start(bf16[16,2048]{1,0:T(8,128)(2,1)S(1)} %get-tuple-element.74), channel_id=1, source_target_pairs={{0,96},{1,97},{2,98},{3,99},{4,100},{5,101},{6,102},{7,103},{8,104... | collective-permute-start | bytes 196616 | tf_op jit(solution)/shard_map/ppermute | solution.py:294
  (40 shorter events, 8.0 us)
Async XLA Ops:
  16.8 11.3 %collective-permute-start = (bf16[1024,2048]{1,0:T(8,128)(2,1)}, bf16[1024,2048]{1,0:T(8,128)(2,1)}, u32[]{:S(2)}, u32[]{:S(2)}) collective-permute-start(bf16[1024,2048]{1,0:T(8,128)(2,1)} %get-tuple-element.39), channel_id=1, source_target_pairs={{0,1},{1,0},{2,3},{3,2},{4,5},{5,4},{6,7},{7,6},{8,9},{9,8},{10,11... | collective-permute-start | bytes 12582920 | tf_op jit(solution)/shard_map/ppermute | solution.py:255
  27.7 16.9 %collective-permute-start.1 = (bf16[1024,2048]{1,0:T(8,128)(2,1)}, bf16[1024,2048]{1,0:T(8,128)(2,1)}, u32[]{:S(2)}, u32[]{:S(2)}) collective-permute-start(bf16[1024,2048]{1,0:T(8,128)(2,1)} %other_product.1), channel_id=1, source_target_pairs={{0,1},{1,0},{2,3},{3,2},{4,5},{5,4},{6,7},{7,6},{8,9},{9,8},{10,11... | collective-permute-start | bytes 12582920 | tf_op jit(solution)/shard_map/ppermute | solution.py:257
  39.6 37.0 %all-to-all-start = ((bf16[4,256,2048]{2,1,0:T(8,128)(2,1)}), bf16[4,256,2048]{2,1,0:T(8,128)(2,1)}, u32[]{:S(2)}, u32[]{:S(2)}) async-start(bf16[4,256,2048]{2,1,0:T(8,128)(2,1)} %get-tuple-element.57), calls=%async_computation | async-start | bytes 8388608 | tf_op jit(solution)/shard_map/all_to_all | solution.py:261
  44.7 32.0 %copy-start = (f32[256,2048]{1,0:T(8,128)S(1)}, f32[256,2048]{1,0:T(8,128)}, u32[]{:S(2)}) copy-start(f32[256,2048]{1,0:T(8,128)} %get-tuple-element.56) | copy-start | bytes 6291460
  60.3 13.7 %collective-permute-start.2 = (bf16[3,512,128]{2,1,0:T(8,128)(2,1)}, bf16[3,512,128]{2,1,0:T(8,128)(2,1)S(1)}, u32[]{:S(2)}, u32[]{:S(2)}) collective-permute-start(bf16[3,512,128]{2,1,0:T(8,128)(2,1)} %get-tuple-element.61), channel_id=1, source_target_pairs={{0,32},{1,33},{2,34},{3,35},{4,36},{5,37},{6,38},{7,39},{8,40},{9,... | collective-permute-start | bytes 1179656 | tf_op jit(solution)/shard_map/ppermute | solution.py:268
  62.4 31.9 %collective-permute-start.5 = (bf16[256,2048]{1,0:T(8,128)(2,1)}, bf16[256,2048]{1,0:T(8,128)(2,1)}, u32[]{:S(2)}, u32[]{:S(2)}) collective-permute-start(bf16[256,2048]{1,0:T(8,128)(2,1)} %get-tuple-element.66), channel_id=1, source_target_pairs={{0,2},{1,9},{2,4},{3,11},{4,6},{5,13},{6,0},{7,15},{8,10},{9,17},{... | collective-permute-start | bytes 3145736 | tf_op jit(solution)/shard_map/ppermute | solution.py:265
  64.1 36.3 %collective-permute-start.6 = (bf16[256,2048]{1,0:T(8,128)(2,1)}, bf16[256,2048]{1,0:T(8,128)(2,1)}, u32[]{:S(2)}, u32[]{:S(2)}) collective-permute-start(bf16[256,2048]{1,0:T(8,128)(2,1)} %get-tuple-element.67), channel_id=1, source_target_pairs={{0,4},{1,17},{2,6},{3,19},{4,0},{5,21},{6,2},{7,23},{8,12},{9,25},... | collective-permute-start | bytes 3145736 | tf_op jit(solution)/shard_map/ppermute | solution.py:265
  66.8 33.6 %collective-permute-start.7 = (bf16[256,2048]{1,0:T(8,128)(2,1)}, bf16[256,2048]{1,0:T(8,128)(2,1)}, u32[]{:S(2)}, u32[]{:S(2)}) collective-permute-start(bf16[256,2048]{1,0:T(8,128)(2,1)} %get-tuple-element.68), channel_id=1, source_target_pairs={{0,6},{1,25},{2,0},{3,27},{4,2},{5,29},{6,4},{7,31},{8,14},{9,1},{... | collective-permute-start | bytes 3145736 | tf_op jit(solution)/shard_map/ppermute | solution.py:265
  68.3 24.6 %collective-permute-start.3 = (bf16[3,512,128]{2,1,0:T(8,128)(2,1)}, bf16[3,512,128]{2,1,0:T(8,128)(2,1)S(1)}, u32[]{:S(2)}, u32[]{:S(2)}) collective-permute-start(bf16[3,512,128]{2,1,0:T(8,128)(2,1)} %get-tuple-element.62), channel_id=1, source_target_pairs={{0,64},{1,65},{2,66},{3,67},{4,68},{5,69},{6,70},{7,71},{8,72},{9,... | collective-permute-start | bytes 1179656 | tf_op jit(solution)/shard_map/ppermute | solution.py:268
  74.0 18.9 %collective-permute-start.4 = (bf16[3,512,128]{2,1,0:T(8,128)(2,1)}, bf16[3,512,128]{2,1,0:T(8,128)(2,1)}, u32[]{:S(2)}, u32[]{:S(2)}) collective-permute-start(bf16[3,512,128]{2,1,0:T(8,128)(2,1)} %get-tuple-element.63), channel_id=1, source_target_pairs={{0,96},{1,97},{2,98},{3,99},{4,100},{5,101},{6,102},{7,103},{8,104... | collective-permute-start | bytes 1179656 | tf_op jit(solution)/shard_map/ppermute | solution.py:268
  80.8 12.2 %copy-start.1 = (bf16[3,512,128]{2,1,0:T(8,128)(2,1)S(1)}, bf16[3,512,128]{2,1,0:T(8,128)(2,1)}, u32[]{:S(2)}) copy-start(bf16[3,512,128]{2,1,0:T(8,128)(2,1)} %get-tuple-element.60) | copy-start | bytes 1179652
  80.8 25.0 %all-to-all-start.1 = ((bf16[16,16,2048]{2,1,0:T(8,128)(2,1)}), bf16[16,16,2048]{2,1,0:T(8,128)(2,1)S(1)}, u32[]{:S(2)}, u32[]{:S(2)}) async-start(bf16[16,16,2048]{2,1,0:T(8,128)(2,1)} %bitcast.12), calls=%async_computation.1 | async-start | bytes 2097152 | tf_op jit(solution)/shard_map/all_to_all | solution.py:276
  106.0 10.6 %collective-permute-start.8 = (bf16[16,2048]{1,0:T(8,128)(2,1)S(1)}, bf16[16,2048]{1,0:T(8,128)(2,1)S(1)}, u32[]{:S(2)}, u32[]{:S(2)}) collective-permute-start(bf16[16,2048]{1,0:T(8,128)(2,1)S(1)} %get-tuple-element.78), channel_id=1, source_target_pairs={{0,32},{1,33},{2,34},{3,35},{4,36},{5,37},{6,38},{7,39},{8,40},{9,... | collective-permute-start | bytes 196616 | tf_op jit(solution)/shard_map/ppermute | solution.py:294
  106.9 9.8 %collective-permute-start.9 = (bf16[16,2048]{1,0:T(8,128)(2,1)S(1)}, bf16[16,2048]{1,0:T(8,128)(2,1)S(1)}, u32[]{:S(2)}, u32[]{:S(2)}) collective-permute-start(bf16[16,2048]{1,0:T(8,128)(2,1)S(1)} %get-tuple-element.78), channel_id=1, source_target_pairs={{0,64},{1,65},{2,66},{3,67},{4,68},{5,69},{6,70},{7,71},{8,72},{9,... | collective-permute-start | bytes 196616 | tf_op jit(solution)/shard_map/ppermute | solution.py:294
  110.5 6.2 %collective-permute-start.10 = (bf16[16,2048]{1,0:T(8,128)(2,1)S(1)}, bf16[16,2048]{1,0:T(8,128)(2,1)S(1)}, u32[]{:S(2)}, u32[]{:S(2)}) collective-permute-start(bf16[16,2048]{1,0:T(8,128)(2,1)S(1)} %get-tuple-element.78), channel_id=1, source_target_pairs={{0,96},{1,97},{2,98},{3,99},{4,100},{5,101},{6,102},{7,103},{8,104... | collective-permute-start | bytes 196616 | tf_op jit(solution)/shard_map/ppermute | solution.py:294
  111.5 18.0 %all-to-all-start.2 = ((bf16[16,16,2048]{2,1,0:T(8,128)(2,1)}), bf16[16,16,2048]{2,1,0:T(8,128)(2,1)S(1)}, u32[]{:S(2)}, u32[]{:S(2)}) async-start(bf16[16,16,2048]{2,1,0:T(8,128)(2,1)} %bitcast.21), calls=%async_computation.2 | async-start | bytes 2097152 | tf_op jit(solution)/shard_map/all_to_all | solution.py:276
  129.8 5.5 %collective-permute-start.11 = (bf16[16,2048]{1,0:T(8,128)(2,1)S(1)}, bf16[16,2048]{1,0:T(8,128)(2,1)S(1)}, u32[]{:S(2)}, u32[]{:S(2)}) collective-permute-start(bf16[16,2048]{1,0:T(8,128)(2,1)S(1)} %get-tuple-element.74), channel_id=1, source_target_pairs={{0,32},{1,33},{2,34},{3,35},{4,36},{5,37},{6,38},{7,39},{8,40},{9,... | collective-permute-start | bytes 196616 | tf_op jit(solution)/shard_map/ppermute | solution.py:294
  130.5 5.8 %collective-permute-start.12 = (bf16[16,2048]{1,0:T(8,128)(2,1)S(1)}, bf16[16,2048]{1,0:T(8,128)(2,1)S(1)}, u32[]{:S(2)}, u32[]{:S(2)}) collective-permute-start(bf16[16,2048]{1,0:T(8,128)(2,1)S(1)} %get-tuple-element.74), channel_id=1, source_target_pairs={{0,64},{1,65},{2,66},{3,67},{4,68},{5,69},{6,70},{7,71},{8,72},{9,... | collective-permute-start | bytes 196616 | tf_op jit(solution)/shard_map/ppermute | solution.py:294
  132.1 4.8 %collective-permute-start.13 = (bf16[16,2048]{1,0:T(8,128)(2,1)S(1)}, bf16[16,2048]{1,0:T(8,128)(2,1)S(1)}, u32[]{:S(2)}, u32[]{:S(2)}) collective-permute-start(bf16[16,2048]{1,0:T(8,128)(2,1)S(1)} %get-tuple-element.74), channel_id=1, source_target_pairs={{0,96},{1,97},{2,98},{3,99},{4,100},{5,101},{6,102},{7,103},{8,104... | collective-permute-start | bytes 196616 | tf_op jit(solution)/shard_map/ppermute | solution.py:294

commit v4 on v3

--- a/solution.py
+++ b/solution.py
@@ -79,33 +79,33 @@
                 pltpu.make_async_copy(other, other_hbm, left.at[1]),
             ]
 
-        def choose(to, core):
+        def choose(to, core, at):
+            for k in range(8):
+                low, high = [
+                    c[at, pl.ds(pl.multiple_of(row_block(t[0], core, 2 * k + i) * 128, 128), 128)] for i in (0, 1)
+                ]
+                to[at, pl.ds(k * 128, 128)] = jnp.concatenate(
+                    [low[:, core * 64:core * 64 + 64], high[:, core * 64:core * 64 + 64]], axis=1
+                )
+
+        def choose_all(core):
             for m in range(parts):
-                at = pl.ds(m * slab, slab)
-                for k in range(8):
-                    low, high = [
-                        c[at, pl.ds(pl.multiple_of(row_block(t[0], core, 2 * k + i) * 128, 128), 128)] for i in (0, 1)
-                    ]
-                    to[at, pl.ds(k * 128, 128)] = jnp.concatenate(
-                        [low[:, core * 64:core * 64 + 64], high[:, core * 64:core * 64 + 64]], axis=1
-                    )
+                piece(m).wait()
+                choose(other, 1 - core, pl.ds(m * slab, slab))
+                choose(mine, core, pl.ds(m * slab, slab))
 
         @pl.when(step == 0)
         def _():
             for m in range(parts):
                 piece(m).start()
-            for m in range(parts):
-                piece(m).wait()
 
             @pl.when((t[0] & 1) == 0)
             def _():
-                choose(other, 1)
-                choose(mine, 0)
+                choose_all(0)
 
             @pl.when((t[0] & 1) == 1)
             def _():
-                choose(other, 0)
-                choose(mine, 1)
+                choose_all(1)
 
             for copy in away():
                 copy.start()
@@ -257,15 +257,15 @@
     received_later = lax.ppermute(theirs, AXES, SWAP)
     (received, mine), theirs = lax.optimization_barrier(((received, mine), theirs))
     own, away = chip_product(shard, mine, out_grad, received, 0, first_cols, True)
-    (own, away), mine = lax.optimization_barrier(((own, away), mine))
+    pieces = (old_master, old_mom1, old_mom2)
+    (own, away), pieces = lax.optimization_barrier(((own, away), pieces))
     arrived = lax.all_to_all(away, AXES, 0, 0, axis_index_groups=ALONG_FIRST, tiled=True)
+    keep, *cut = windows(old_lengths[0], group, pieces)
+    (keep, cut), mine = lax.optimization_barrier(((keep, cut), mine))
+    cut = [lax.ppermute(cut[k - 1], AXES, THIRD[k]) for k in (1, 2, 3)]
     own_later, *away = chip_product(shard, mine, out_grad, received_later, first_cols, second_cols, False)
-    pieces = (old_master, old_mom1, old_mom2)
-    pieces, own_later = lax.optimization_barrier((pieces, own_later))
+    cut, arrived, own_later = lax.optimization_barrier((cut, arrived, own_later))
     arrived_later = [lax.ppermute(away[k - 1], AXES, FIRST[k]) for k in (1, 2, 3)]
-    keep, *cut = windows(old_lengths[0], group, pieces)
-    (keep, cut), own = lax.optimization_barrier(((keep, cut), own))
-    cut = [lax.ppermute(cut[k - 1], AXES, THIRD[k]) for k in (1, 2, 3)]
     state = sum([value.astype(f32) for value in cut], keep.astype(f32)).reshape(3, ROWS // N_GRP, width)
 
     def first_sum(own, arrived):
@@ -285,7 +285,6 @@
     place = jnp.where(shard[0] % 2 == 0, shard[0] // 2 % 4, shard[0] // 8)
     summed = first_sum(own, [jnp.where(place == k, 0.0, arrived[k].astype(f32)) for k in range(4)])
     summed, own_later = lax.optimization_barrier((summed, own_later))
-    own_later, state = lax.optimization_barrier((own_later, state))
     terms = owners(summed)
     summed_later = first_sum(own_later, arrived_later)
     summed_later, terms = lax.optimization_barrier((summed_later, terms))
@@ -297,13 +296,10 @@
             whole = lax.dynamic_update_index_in_dim(whole, part, (group[0] - k) % N_GRP, 0)
         return whole.reshape(ROWS, -1)
 
-    result = step(state[:, :, :first_cols], terms)
-    weights = to_groups(result[0].astype(bf16))
-    weights, terms_later = lax.optimization_barrier((weights, terms_later))
-    result_later = step(state[:, :, first_cols:], terms_later)
-    weights = [weights, to_groups(result_later[0].astype(bf16))]
-    outputs = [*zip(result, result_later), weights]
-    return tuple(jnp.concatenate(parts, axis=1)[None] for parts in outputs)
+    results = [step(state[:, :, :first_cols], terms), step(state[:, :, first_cols:], terms_later)]
+    master_new, first_new, second_new = [jnp.concatenate(parts, axis=1) for parts in zip(*results)]
+    weights = to_groups(master_new.astype(bf16))
+    return (master_new[None], first_new[None], second_new[None], weights[None])
 
 
 def solution(mesh):

time: 138 us -> 136 us (0.986)
  starting transfers between devices: 46.1 us -> 37.1 us
  waiting for transfers between devices: 23.9 us -> 30 us
  local copies, waits for them, and re-layouts: 0.25 us -> 3.09 us
  Pallas kernels: 54 us -> 52.5 us
    ppermute x3, waiting for transfers between devices: 6.15 us -> 16.3 us  [local(): lax.ppermute(away[k - 1], AXES, FIRST[k])]
    ppermute x6 -> x3, starting transfers between devices: 9.3 us -> 4.38 us  [to_groups(): parts = [part] + [lax.ppermute(part, AXES, THIRD[k]) for k in (1, 2, 3)]]
    all_to_all x2, waiting for transfers between devices: 14 us -> 11.2 us  [owners(): lax.all_to_all(summed, AXES, 0, 0, axis_index_groups=SECOND, tiled=True)]
    all_to_all x2, starting transfers between devices: 17.1 us -> 14.6 us  [owners(): lax.all_to_all(summed, AXES, 0, 0, axis_index_groups=SECOND, tiled=True)]
    ppermute x3, waiting for transfers between devices: 2.18 us -> 0.01 us  [local(): cut = [lax.ppermute(cut[k - 1], AXES, THIRD[k]) for k in (1, 2, 3)]]
    unnamed x4 -> x14, local copies, waits for them, and re-layouts: 0.01 us -> 1.74 us
    ppermute x3, starting transfers between devices: 8.25 us -> 6.63 us  [local(): cut = [lax.ppermute(cut[k - 1], AXES, THIRD[k]) for k in (1, 2, 3)]]
  transfers between devices with their start and end apart: 17 -> 14, of which waited for: 6 -> 4; matrix products, arithmetic and copies ran while one was open for 8% -> 9% of each run, Pallas kernels for 27% -> 28%
where the time goes in v4:
time: 136 us
  Pallas kernels  52.5 us (39%)
  starting transfers between devices  37.1 us (27%)
  waiting for transfers between devices  30 us (22%)
  other arithmetic  11.9 us (9%)
  local copies, waits for them, and re-layouts  3.09 us (2%)
    pallas_call x2, Pallas kernels, chip_product(): pl.pallas_call(body, grid_spec=pltpu.PrefetchScalarGridSpec(num_scalar_pr...  22.7 us
    ppermute x3, waiting for transfers between devices, local(): lax.ppermute(away[k - 1], AXES, FIRST[k])  16.3 us
    pallas_call x1, Pallas kernels, first_product(): pl.pallas_call(body, grid_spec=pltpu.PrefetchScalarGridSpec(num_scalar_pr...  14.8 us
    all_to_all x2, starting transfers between devices, owners(): lax.all_to_all(summed, AXES, 0, 0, axis_index_groups=SECOND, tiled=True)  14.6 us
    all_to_all x2, waiting for transfers between devices, owners(): lax.all_to_all(summed, AXES, 0, 0, axis_index_groups=SECOND, tiled=True)  11.2 us
    pallas_call x1, Pallas kernels, other_product(): pl.pallas_call(body, grid=(cols // TILE,), in_specs=[pl.BlockSpec((tokens...  10.8 us
    convert_element_type x2, other arithmetic, first_sum(): return sum([value.astype(f32) for value in arrived], own).astype(bf16)  7.63 us
    ppermute x3, starting transfers between devices, local(): cut = [lax.ppermute(cut[k - 1], AXES, THIRD[k]) for k in (1, 2, 3)]  6.63 us
  transfers between devices with their start and end apart: 14, of which 4 were waited for; matrix products, arithmetic and copies ran while one was open for 9% of the time, Pallas kernels for 28%

profile of v4, /device:TPU:0, one launch (start us, length us, event | category | flops | bytes accessed | tf_op | source)
XLA Modules:
  0.0 135.5 jit_solution(7877696672500124581)
XLA Ops:
  0.6 14.8 %first_product.1 = (bf16[1024,2048]{1,0:T(8,128)(2,1)}, bf16[1536,1024]{1,0:T(8,128)(2,1)}, bf16[1536,1024]{1,0:T(8,128)(2,1)}) custom-call(s32[1]{0:T(128)} %bitcast.2.t, bf16[1536,2048]{1,0:T(8,128)(2,1)} %c_hbm.1, bf16[1536,4096]{1,0:T(8,128)(2,1)} %g.7), custom_call_target="tpu_custom_call" | custom-call | flops 402653184 | bytes 655360 | tf_op jit(solution)/shard_map/first_product/pallas_call | solution.py:121
  15.6 10.8 %other_product.1 = bf16[1024,2048]{1,0:T(8,128)(2,1)} custom-call(bf16[1536,1024]{1,0:T(8,128)(2,1)} %get-tuple-element.40.c, bf16[1536,4096]{1,0:T(8,128)(2,1)} %g.7), custom_call_target="tpu_custom_call" | custom-call | flops 402653184 | bytes 655360 | tf_op jit(solution)/shard_map/other_product/pallas_call | solution.py:153
  26.8 11.4 %chip_product.2 = (f32[256,2048]{1,0:T(8,128)}, bf16[4,256,2048]{2,1,0:T(8,128)(2,1)}) custom-call(s32[1]{0:T(128)} %bitcast.2.t, bf16[1536,1024]{1,0:T(8,128)(2,1)} %get-tuple-element.57.c, bf16[1536,4096]{1,0:T(8,128)(2,1)} %g.7, bf16[1024,2048]{1,0:T(8,128)(2,1)} %collective-permute-done.r), custom_call_target="tpu_custom_call" | custom-call | flops 402653184 | bytes 655360 | tf_op jit(solution)/shard_map/chip_product/pallas_call | solution.py:188
  38.3 5.1 %all-to-all-start = ((bf16[4,256,2048]{2,1,0:T(8,128)(2,1)}), bf16[4,256,2048]{2,1,0:T(8,128)(2,1)}, u32[]{:S(2)}, u32[]{:S(2)}) async-start(bf16[4,256,2048]{2,1,0:T(8,128)(2,1)} %get-tuple-element.56), calls=%async_computation | async-start | bytes 8388608 | tf_op jit(solution)/shard_map/all_to_all | solution.py:262
  43.3 4.2 %windows.1 = (bf16[3,512,128]{2,1,0:T(8,128)(2,1)}, bf16[3,512,128]{2,1,0:T(8,128)(2,1)}, bf16[3,512,128]{2,1,0:T(8,128)(2,1)}, bf16[3,512,128]{2,1,0:T(8,128)(2,1)}) custom-call(s32[4]{0:T(128)} %bitcast.79, s32[1]{0:T(128)} %bitcast.1.g, f32[1024,128]{1,0:T(8,128)} %bitcast.76, f32[1024,128]{1,0:T(8,128)} %bitcast.77, f32[1024,128]{1,0:T(8,128)} %bitcast.78), custom_call_target="tpu_custom_call" | custom-call | flops 10000000 | bytes 4000000 | tf_op jit(solution)/shard_map/windows/pallas_call | solution.py:233
  47.5 2.0 %collective-permute-start.1 = (bf16[3,512,128]{2,1,0:T(8,128)(2,1)}, bf16[3,512,128]{2,1,0:T(8,128)(2,1)S(1)}, u32[]{:S(2)}, u32[]{:S(2)}) collective-permute-start(bf16[3,512,128]{2,1,0:T(8,128)(2,1)} %get-tuple-element.53), channel_id=1, source_target_pairs={{0,32},{1,33},{2,34},{3,35},{4,36},{5,37},{6,38},{7,39},{8,40},{9,... | collective-permute-start | bytes 1179656 | tf_op jit(solution)/shard_map/ppermute | solution.py:265
  49.5 3.6 %collective-permute-start.2 = (bf16[3,512,128]{2,1,0:T(8,128)(2,1)}, bf16[3,512,128]{2,1,0:T(8,128)(2,1)S(1)}, u32[]{:S(2)}, u32[]{:S(2)}) collective-permute-start(bf16[3,512,128]{2,1,0:T(8,128)(2,1)} %get-tuple-element.54), channel_id=1, source_target_pairs={{0,64},{1,65},{2,66},{3,67},{4,68},{5,69},{6,70},{7,71},{8,72},{9,... | collective-permute-start | bytes 1179656 | tf_op jit(solution)/shard_map/ppermute | solution.py:265
  53.1 1.0 collective-permute-start.3
  54.1 11.3 %chip_product.3 = (f32[256,2048]{1,0:T(8,128)}, bf16[256,2048]{1,0:T(8,128)(2,1)}, bf16[256,2048]{1,0:T(8,128)(2,1)}, bf16[256,2048]{1,0:T(8,128)(2,1)}) custom-call(s32[1]{0:T(128)} %bitcast.2.t, bf16[1536,1024]{1,0:T(8,128)(2,1)} %get-tuple-element.57.c, bf16[1536,4096]{1,0:T(8,128)(2,1)} %g.7, bf16[1024,2048]{1,0:T(8,128)(2,1)} %collective-permute-done.4.r), custom_call_target="tpu_custom_call" | custom-call | flops 402653184 | bytes 655360 | tf_op jit(solution)/shard_map/chip_product/pallas_call | solution.py:188
  65.4 1.8 %collective-permute-start.5 = (bf16[256,2048]{1,0:T(8,128)(2,1)}, bf16[256,2048]{1,0:T(8,128)(2,1)}, u32[]{:S(2)}, u32[]{:S(2)}) collective-permute-start(bf16[256,2048]{1,0:T(8,128)(2,1)} %get-tuple-element.66), channel_id=1, source_target_pairs={{0,2},{1,9},{2,4},{3,11},{4,6},{5,13},{6,0},{7,15},{8,10},{9,17},{... | collective-permute-start | bytes 3145736 | tf_op jit(solution)/shard_map/ppermute | solution.py:268
  67.2 2.6 %collective-permute-start.6 = (bf16[256,2048]{1,0:T(8,128)(2,1)}, bf16[256,2048]{1,0:T(8,128)(2,1)}, u32[]{:S(2)}, u32[]{:S(2)}) collective-permute-start(bf16[256,2048]{1,0:T(8,128)(2,1)} %get-tuple-element.67), channel_id=1, source_target_pairs={{0,4},{1,17},{2,6},{3,19},{4,0},{5,21},{6,2},{7,23},{8,12},{9,25},... | collective-permute-start | bytes 3145736 | tf_op jit(solution)/shard_map/ppermute | solution.py:268
  69.9 1.5 %collective-permute-start.7 = (bf16[256,2048]{1,0:T(8,128)(2,1)}, bf16[256,2048]{1,0:T(8,128)(2,1)}, u32[]{:S(2)}, u32[]{:S(2)}) collective-permute-start(bf16[256,2048]{1,0:T(8,128)(2,1)} %get-tuple-element.68), channel_id=1, source_target_pairs={{0,6},{1,25},{2,0},{3,27},{4,2},{5,29},{6,4},{7,31},{8,14},{9,1},{... | collective-permute-start | bytes 3145736 | tf_op jit(solution)/shard_map/ppermute | solution.py:268
  72.3 4.1 %fusion = bf16[256,2048]{1,0:T(8,128)(2,1)} fusion(f32[256,2048]{1,0:T(8,128)S(1)} %copy-done.1, bf16[4,256,2048]{2,1,0:T(8,128)(2,1)} %all-to-all-done, pred[]{:T(512)S(6)} %eq.26, pred[]{:T(512)S(6)} %eq.25, pred[]{:T(512)S(6)} %eq.24, pred[]{:T(512)S(6)} %eq.23), kind=kLoop, calls=%fused_computation.1 | loop fusion | flops 6815744 | bytes 7340036 | tf_op jit(solution)/shard_map/convert_element_type | solution.py:272
  76.4 7.0 %all-to-all-start.1 = ((bf16[16,16,2048]{2,1,0:T(8,128)(2,1)}), bf16[16,16,2048]{2,1,0:T(8,128)(2,1)S(1)}, u32[]{:S(2)}, u32[]{:S(2)}) async-start(bf16[16,16,2048]{2,1,0:T(8,128)(2,1)} %bitcast.12), calls=%async_computation.1 | async-start | bytes 2097152 | tf_op jit(solution)/shard_map/all_to_all | solution.py:276
  83.5 16.3 %collective-permute-done.6 = bf16[256,2048]{1,0:T(8,128)(2,1)} collective-permute-done((bf16[256,2048]{1,0:T(8,128)(2,1)}, bf16[256,2048]{1,0:T(8,128)(2,1)}, u32[]{:S(2)}, u32[]{:S(2)}) %collective-permute-start.6) | collective-permute-done | bytes 1048608 | tf_op jit(solution)/shard_map/ppermute | solution.py:268
  99.8 3.5 %add_convert_fusion = bf16[256,2048]{1,0:T(8,128)(2,1)} fusion(bf16[256,2048]{1,0:T(8,128)(2,1)} %collective-permute-done.7, bf16[256,2048]{1,0:T(8,128)(2,1)} %collective-permute-done.6, f32[256,2048]{1,0:T(8,128)S(1)} %copy-done, bf16[256,2048]{1,0:T(8,128)(2,1)} %collective-permute-done.5), kind=kLoop, calls=%fused_computation.7 | loop fusion | flops 3670016 | bytes 6291456 | tf_op jit(solution)/shard_map/convert_element_type | solution.py:272
  103.3 7.6 %all-to-all-start.2 = ((bf16[16,16,2048]{2,1,0:T(8,128)(2,1)}), bf16[16,16,2048]{2,1,0:T(8,128)(2,1)S(1)}, u32[]{:S(2)}, u32[]{:S(2)}) async-start(bf16[16,16,2048]{2,1,0:T(8,128)(2,1)} %bitcast.16), calls=%async_computation.2 | async-start | bytes 2097152 | tf_op jit(solution)/shard_map/all_to_all | solution.py:276
  111.0 2.1 %convert_add_fusion = f32[3,512,128]{2,1,0:T(8,128)} fusion(bf16[3,512,128]{2,1,0:T(8,128)(2,1)} %copy-done.6, bf16[3,512,128]{2,1,0:T(8,128)(2,1)S(1)} %copy-done.5, bf16[3,512,128]{2,1,0:T(8,128)(2,1)S(1)} %collective-permute-done.1, bf16[3,512,128]{2,1,0:T(8,128)(2,1)S(1)} %copy-done.3), kind=kLoop, calls=%fused_computation.8 | loop fusion | flops 1376256 | bytes 2359296 | tf_op jit(solution)/shard_map/add | solution.py:269
  113.0 1.3 reshape.98
  114.5 11.2 %all-to-all-done.2 = bf16[16,16,2048]{2,1,0:T(8,128)(2,1)S(1)} async-done(((bf16[16,16,2048]{2,1,0:T(8,128)(2,1)}), bf16[16,16,2048]{2,1,0:T(8,128)(2,1)S(1)}, u32[]{:S(2)}, u32[]{:S(2)}) %all-to-all-start.2) | async-done | bytes 1048608 | tf_op jit(solution)/shard_map/all_to_all | solution.py:276
  126.2 0.9 collective-permute-start.8
  127.0 2.3 %collective-permute-start.9 = (bf16[16,4096]{1,0:T(8,128)(2,1)S(1)}, bf16[16,4096]{1,0:T(8,128)(2,1)S(1)}, u32[]{:S(2)}, u32[]{:S(2)}) collective-permute-start(bf16[16,4096]{1,0:T(8,128)(2,1)S(1)} %fusion.1), channel_id=1, source_target_pairs={{0,64},{1,65},{2,66},{3,67},{4,68},{5,69},{6,70},{7,71},{8,72},{9,... | collective-permute-start | bytes 393224 | tf_op jit(solution)/shard_map/ppermute | solution.py:293
  129.4 1.2 collective-permute-start.10
  132.2 1.8 %collective-permute-done.8 = bf16[16,4096]{1,0:T(8,128)(2,1)S(1)} collective-permute-done((bf16[16,4096]{1,0:T(8,128)(2,1)S(1)}, bf16[16,4096]{1,0:T(8,128)(2,1)S(1)}, u32[]{:S(2)}, u32[]{:S(2)}) %collective-permute-start.8) | collective-permute-done | bytes 131104 | tf_op jit(solution)/shard_map/ppermute | solution.py:293
  (39 shorter events, 5.3 us)
Async XLA Ops:
  15.5 11.3 %collective-permute-start = (bf16[1024,2048]{1,0:T(8,128)(2,1)}, bf16[1024,2048]{1,0:T(8,128)(2,1)}, u32[]{:S(2)}, u32[]{:S(2)}) collective-permute-start(bf16[1024,2048]{1,0:T(8,128)(2,1)} %get-tuple-element.38), channel_id=1, source_target_pairs={{0,1},{1,0},{2,3},{3,2},{4,5},{5,4},{6,7},{7,6},{8,9},{9,8},{10,11... | collective-permute-start | bytes 12582920 | tf_op jit(solution)/shard_map/ppermute | solution.py:255
  26.4 27.8 %collective-permute-start.4 = (bf16[1024,2048]{1,0:T(8,128)(2,1)}, bf16[1024,2048]{1,0:T(8,128)(2,1)}, u32[]{:S(2)}, u32[]{:S(2)}) collective-permute-start(bf16[1024,2048]{1,0:T(8,128)(2,1)} %other_product.1), channel_id=1, source_target_pairs={{0,1},{1,0},{2,3},{3,2},{4,5},{5,4},{6,7},{7,6},{8,9},{9,8},{10,11... | collective-permute-start | bytes 12582920 | tf_op jit(solution)/shard_map/ppermute | solution.py:257
  38.3 33.1 %all-to-all-start = ((bf16[4,256,2048]{2,1,0:T(8,128)(2,1)}), bf16[4,256,2048]{2,1,0:T(8,128)(2,1)}, u32[]{:S(2)}, u32[]{:S(2)}) async-start(bf16[4,256,2048]{2,1,0:T(8,128)(2,1)} %get-tuple-element.56), calls=%async_computation | async-start | bytes 8388608 | tf_op jit(solution)/shard_map/all_to_all | solution.py:262
  47.5 24.8 %copy-start.1 = (f32[256,2048]{1,0:T(8,128)S(1)}, f32[256,2048]{1,0:T(8,128)}, u32[]{:S(2)}) copy-start(f32[256,2048]{1,0:T(8,128)} %get-tuple-element.62) | copy-start | bytes 6291460
  47.5 22.4 %collective-permute-start.1 = (bf16[3,512,128]{2,1,0:T(8,128)(2,1)}, bf16[3,512,128]{2,1,0:T(8,128)(2,1)S(1)}, u32[]{:S(2)}, u32[]{:S(2)}) collective-permute-start(bf16[3,512,128]{2,1,0:T(8,128)(2,1)} %get-tuple-element.53), channel_id=1, source_target_pairs={{0,32},{1,33},{2,34},{3,35},{4,36},{5,37},{6,38},{7,39},{8,40},{9,... | collective-permute-start | bytes 1179656 | tf_op jit(solution)/shard_map/ppermute | solution.py:265
  49.5 21.8 %collective-permute-start.2 = (bf16[3,512,128]{2,1,0:T(8,128)(2,1)}, bf16[3,512,128]{2,1,0:T(8,128)(2,1)S(1)}, u32[]{:S(2)}, u32[]{:S(2)}) collective-permute-start(bf16[3,512,128]{2,1,0:T(8,128)(2,1)} %get-tuple-element.54), channel_id=1, source_target_pairs={{0,64},{1,65},{2,66},{3,67},{4,68},{5,69},{6,70},{7,71},{8,72},{9,... | collective-permute-start | bytes 1179656 | tf_op jit(solution)/shard_map/ppermute | solution.py:265
  53.1 18.3 %collective-permute-start.3 = (bf16[3,512,128]{2,1,0:T(8,128)(2,1)}, bf16[3,512,128]{2,1,0:T(8,128)(2,1)S(1)}, u32[]{:S(2)}, u32[]{:S(2)}) collective-permute-start(bf16[3,512,128]{2,1,0:T(8,128)(2,1)} %get-tuple-element.55), channel_id=1, source_target_pairs={{0,96},{1,97},{2,98},{3,99},{4,100},{5,101},{6,102},{7,103},{8,104... | collective-permute-start | bytes 1179656 | tf_op jit(solution)/shard_map/ppermute | solution.py:265
  65.4 18.0 %collective-permute-start.5 = (bf16[256,2048]{1,0:T(8,128)(2,1)}, bf16[256,2048]{1,0:T(8,128)(2,1)}, u32[]{:S(2)}, u32[]{:S(2)}) collective-permute-start(bf16[256,2048]{1,0:T(8,128)(2,1)} %get-tuple-element.66), channel_id=1, source_target_pairs={{0,2},{1,9},{2,4},{3,11},{4,6},{5,13},{6,0},{7,15},{8,10},{9,17},{... | collective-permute-start | bytes 3145736 | tf_op jit(solution)/shard_map/ppermute | solution.py:268
  67.2 32.6 %collective-permute-start.6 = (bf16[256,2048]{1,0:T(8,128)(2,1)}, bf16[256,2048]{1,0:T(8,128)(2,1)}, u32[]{:S(2)}, u32[]{:S(2)}) collective-permute-start(bf16[256,2048]{1,0:T(8,128)(2,1)} %get-tuple-element.67), channel_id=1, source_target_pairs={{0,4},{1,17},{2,6},{3,19},{4,0},{5,21},{6,2},{7,23},{8,12},{9,25},... | collective-permute-start | bytes 3145736 | tf_op jit(solution)/shard_map/ppermute | solution.py:268
  69.9 29.9 %collective-permute-start.7 = (bf16[256,2048]{1,0:T(8,128)(2,1)}, bf16[256,2048]{1,0:T(8,128)(2,1)}, u32[]{:S(2)}, u32[]{:S(2)}) collective-permute-start(bf16[256,2048]{1,0:T(8,128)(2,1)} %get-tuple-element.68), channel_id=1, source_target_pairs={{0,6},{1,25},{2,0},{3,27},{4,2},{5,29},{6,4},{7,31},{8,14},{9,1},{... | collective-permute-start | bytes 3145736 | tf_op jit(solution)/shard_map/ppermute | solution.py:268
  71.3 0.8 copy-start.4
  71.3 1.0 copy-start.6
  76.4 23.4 %copy-start = (f32[256,2048]{1,0:T(8,128)S(1)}, f32[256,2048]{1,0:T(8,128)}, u32[]{:S(2)}) copy-start(f32[256,2048]{1,0:T(8,128)} %get-tuple-element.65) | copy-start | bytes 6291460
  76.4 26.9 %all-to-all-start.1 = ((bf16[16,16,2048]{2,1,0:T(8,128)(2,1)}), bf16[16,16,2048]{2,1,0:T(8,128)(2,1)S(1)}, u32[]{:S(2)}, u32[]{:S(2)}) async-start(bf16[16,16,2048]{2,1,0:T(8,128)(2,1)} %bitcast.12), calls=%async_computation.1 | async-start | bytes 2097152 | tf_op jit(solution)/shard_map/all_to_all | solution.py:276
  103.3 7.7 %copy-start.3 = (bf16[3,512,128]{2,1,0:T(8,128)(2,1)S(1)}, bf16[3,512,128]{2,1,0:T(8,128)(2,1)}, u32[]{:S(2)}) copy-start(bf16[3,512,128]{2,1,0:T(8,128)(2,1)} %get-tuple-element.52) | copy-start | bytes 1179652
  103.3 7.7 %copy-start.5 = (bf16[3,512,128]{2,1,0:T(8,128)(2,1)S(1)}, bf16[3,512,128]{2,1,0:T(8,128)(2,1)}, u32[]{:S(2)}) copy-start(bf16[3,512,128]{2,1,0:T(8,128)(2,1)} %copy-done.4) | copy-start | bytes 1179652
  103.3 22.3 %all-to-all-start.2 = ((bf16[16,16,2048]{2,1,0:T(8,128)(2,1)}), bf16[16,16,2048]{2,1,0:T(8,128)(2,1)S(1)}, u32[]{:S(2)}, u32[]{:S(2)}) async-start(bf16[16,16,2048]{2,1,0:T(8,128)(2,1)} %bitcast.16), calls=%async_computation.2 | async-start | bytes 2097152 | tf_op jit(solution)/shard_map/all_to_all | solution.py:276
  126.2 7.8 %collective-permute-start.8 = (bf16[16,4096]{1,0:T(8,128)(2,1)S(1)}, bf16[16,4096]{1,0:T(8,128)(2,1)S(1)}, u32[]{:S(2)}, u32[]{:S(2)}) collective-permute-start(bf16[16,4096]{1,0:T(8,128)(2,1)S(1)} %fusion.1), channel_id=1, source_target_pairs={{0,32},{1,33},{2,34},{3,35},{4,36},{5,37},{6,38},{7,39},{8,40},{9,... | collective-permute-start | bytes 393224 | tf_op jit(solution)/shard_map/ppermute | solution.py:293
  127.0 7.0 %collective-permute-start.9 = (bf16[16,4096]{1,0:T(8,128)(2,1)S(1)}, bf16[16,4096]{1,0:T(8,128)(2,1)S(1)}, u32[]{:S(2)}, u32[]{:S(2)}) collective-permute-start(bf16[16,4096]{1,0:T(8,128)(2,1)S(1)} %fusion.1), channel_id=1, source_target_pairs={{0,64},{1,65},{2,66},{3,67},{4,68},{5,69},{6,70},{7,71},{8,72},{9,... | collective-permute-start | bytes 393224 | tf_op jit(solution)/shard_map/ppermute | solution.py:293
  129.4 5.3 %collective-permute-start.10 = (bf16[16,4096]{1,0:T(8,128)(2,1)S(1)}, bf16[16,4096]{1,0:T(8,128)(2,1)S(1)}, u32[]{:S(2)}, u32[]{:S(2)}) collective-permute-start(bf16[16,4096]{1,0:T(8,128)(2,1)S(1)} %fusion.1), channel_id=1, source_target_pairs={{0,96},{1,97},{2,98},{3,99},{4,100},{5,101},{6,102},{7,103},{8,104... | collective-permute-start | bytes 393224 | tf_op jit(solution)/shard_map/ppermute | solution.py:293
  134.7 0.8 copy-start.2

commit v5 on v4

--- a/solution.py
+++ b/solution.py
@@ -63,7 +63,7 @@
 
 def first_product(shard, context, out_grad, start, cols):
     tokens, height = context.shape
-    half, parts = height // 2, 4
+    half, parts = height // 2, 8
     slab = tokens // parts
 
     def body(t, c_hbm, g, out, mine_hbm, other_hbm, c, mine, other, arrived, left):
@@ -262,11 +262,11 @@
     arrived = lax.all_to_all(away, AXES, 0, 0, axis_index_groups=ALONG_FIRST, tiled=True)
     keep, *cut = windows(old_lengths[0], group, pieces)
     (keep, cut), mine = lax.optimization_barrier(((keep, cut), mine))
+    own_later, *away = chip_product(shard, mine, out_grad, received_later, first_cols, second_cols, False)
+    own_later, cut = lax.optimization_barrier((own_later, cut))
+    arrived_later = [lax.ppermute(away[k - 1], AXES, FIRST[k]) for k in (1, 2, 3)]
     cut = [lax.ppermute(cut[k - 1], AXES, THIRD[k]) for k in (1, 2, 3)]
-    own_later, *away = chip_product(shard, mine, out_grad, received_later, first_cols, second_cols, False)
-    cut, arrived, own_later = lax.optimization_barrier((cut, arrived, own_later))
-    arrived_later = [lax.ppermute(away[k - 1], AXES, FIRST[k]) for k in (1, 2, 3)]
-    state = sum([value.astype(f32) for value in cut], keep.astype(f32)).reshape(3, ROWS // N_GRP, width)
+    cut[0], cut[2], arrived, own_later = lax.optimization_barrier((cut[0], cut[2], arrived, own_later))
 
     def first_sum(own, arrived):
         return sum([value.astype(f32) for value in arrived], own).astype(bf16)
@@ -283,9 +283,10 @@
         return master - step_size * first_new / (jnp.sqrt(second_new) + epsilon), first_new, second_new
 
     place = jnp.where(shard[0] % 2 == 0, shard[0] // 2 % 4, shard[0] // 8)
-    summed = first_sum(own, [jnp.where(place == k, 0.0, arrived[k].astype(f32)) for k in range(4)])
-    summed, own_later = lax.optimization_barrier((summed, own_later))
+    summed = first_sum(own, [lax.dynamic_index_in_dim(arrived, (place + k) % 4, 0, False) for k in (1, 2, 3)])
+    summed, own_later, cut[1] = lax.optimization_barrier((summed, own_later, cut[1]))
     terms = owners(summed)
+    state = sum([value.astype(f32) for value in cut], keep.astype(f32)).reshape(3, ROWS // N_GRP, width)
     summed_later = first_sum(own_later, arrived_later)
     summed_later, terms = lax.optimization_barrier((summed_later, terms))
     terms_later = owners(summed_later)

time: 136 us -> 136 us (level)
  starting transfers between devices: 37.1 us -> 31.7 us
  waiting for transfers between devices: 30 us -> 35.3 us
    ppermute x3, waiting for transfers between devices: 0.01 us -> 11.3 us  [local(): cut = [lax.ppermute(cut[k - 1], AXES, THIRD[k]) for k in (1, 2, 3)]]
    ppermute x3, waiting for transfers between devices: 16.3 us -> 7.04 us  [local(): lax.ppermute(away[k - 1], AXES, FIRST[k])]
    all_to_all x2, starting transfers between devices: 14.6 us -> 11.1 us  [owners(): lax.all_to_all(summed, AXES, 0, 0, axis_index_groups=SECOND, tiled=True)]
    all_to_all x2, waiting for transfers between devices: 11.2 us -> 13.8 us  [owners(): lax.all_to_all(summed, AXES, 0, 0, axis_index_groups=SECOND, tiled=True)]
  transfers between devices with their start and end apart: 14 -> 14, of which waited for: 4 -> 8; matrix products, arithmetic and copies ran while one was open for 9% -> 8% of each run, Pallas kernels for 28% -> 28%
where the time goes in v5:
time: 136 us; the launch traced here: 135 us
  Pallas kernels  52.4 us (39%)
  waiting for transfers between devices  35.3 us (26%)
  starting transfers between devices  31.7 us (23%)
  other arithmetic  11.3 us (8%)
  local copies, waits for them, and re-layouts  2.92 us (2%)
    pallas_call x2, Pallas kernels, chip_product(): pl.pallas_call(body, grid_spec=pltpu.PrefetchScalarGridSpec(num_scalar_pr...  22.9 us
    pallas_call x1, Pallas kernels, first_product(): pl.pallas_call(body, grid_spec=pltpu.PrefetchScalarGridSpec(num_scalar_pr...  14.6 us
    all_to_all x2, waiting for transfers between devices, owners(): lax.all_to_all(summed, AXES, 0, 0, axis_index_groups=SECOND, tiled=True)  13.8 us
    ppermute x3, waiting for transfers between devices, local(): cut = [lax.ppermute(cut[k - 1], AXES, THIRD[k]) for k in (1, 2, 3)]  11.3 us
    all_to_all x2, starting transfers between devices, owners(): lax.all_to_all(summed, AXES, 0, 0, axis_index_groups=SECOND, tiled=True)  11.1 us
    pallas_call x1, Pallas kernels, other_product(): pl.pallas_call(body, grid=(cols // TILE,), in_specs=[pl.BlockSpec((tokens...  10.8 us
    ppermute x3, waiting for transfers between devices, local(): lax.ppermute(away[k - 1], AXES, FIRST[k])  7.04 us
    convert_element_type x2, other arithmetic, first_sum(): return sum([value.astype(f32) for value in arrived], own).astype(bf16)  6.98 us
  transfers between devices with their start and end apart: 14, of which 8 were waited for; matrix products, arithmetic and copies ran while one was open for 8% of the time, Pallas kernels for 28%

profile of v5, /device:TPU:0, one launch (start us, length us, event | category | flops | bytes accessed | tf_op | source)
XLA Modules:
  0.0 134.5 jit_solution(4328303975526714967)
XLA Ops:
  0.6 14.6 %first_product.1 = (bf16[1024,2048]{1,0:T(8,128)(2,1)}, bf16[1536,1024]{1,0:T(8,128)(2,1)}, bf16[1536,1024]{1,0:T(8,128)(2,1)}) custom-call(s32[1]{0:T(128)} %bitcast.2.t, bf16[1536,2048]{1,0:T(8,128)(2,1)} %c_hbm.1, bf16[1536,4096]{1,0:T(8,128)(2,1)} %g.7), custom_call_target="tpu_custom_call" | custom-call | flops 402653184 | bytes 655360 | tf_op jit(solution)/shard_map/first_product/pallas_call | solution.py:121
  15.4 10.8 %other_product.1 = bf16[1024,2048]{1,0:T(8,128)(2,1)} custom-call(bf16[1536,1024]{1,0:T(8,128)(2,1)} %get-tuple-element.44.c, bf16[1536,4096]{1,0:T(8,128)(2,1)} %g.7), custom_call_target="tpu_custom_call" | custom-call | flops 402653184 | bytes 655360 | tf_op jit(solution)/shard_map/other_product/pallas_call | solution.py:153
  26.6 11.4 %chip_product.2 = (f32[256,2048]{1,0:T(8,128)}, bf16[4,256,2048]{2,1,0:T(8,128)(2,1)}) custom-call(s32[1]{0:T(128)} %bitcast.2.t, bf16[1536,1024]{1,0:T(8,128)(2,1)} %get-tuple-element.57.c, bf16[1536,4096]{1,0:T(8,128)(2,1)} %g.7, bf16[1024,2048]{1,0:T(8,128)(2,1)} %collective-permute-done.r), custom_call_target="tpu_custom_call" | custom-call | flops 402653184 | bytes 655360 | tf_op jit(solution)/shard_map/chip_product/pallas_call | solution.py:188
  38.1 5.1 %all-to-all-start = ((bf16[4,256,2048]{2,1,0:T(8,128)(2,1)}), bf16[4,256,2048]{2,1,0:T(8,128)(2,1)}, u32[]{:S(2)}, u32[]{:S(2)}) async-start(bf16[4,256,2048]{2,1,0:T(8,128)(2,1)} %get-tuple-element.64), calls=%async_computation | async-start | bytes 8388608 | tf_op jit(solution)/shard_map/all_to_all | solution.py:262
  43.1 4.1 %windows.1 = (bf16[3,512,128]{2,1,0:T(8,128)(2,1)}, bf16[3,512,128]{2,1,0:T(8,128)(2,1)}, bf16[3,512,128]{2,1,0:T(8,128)(2,1)}, bf16[3,512,128]{2,1,0:T(8,128)(2,1)}) custom-call(s32[4]{0:T(128)} %bitcast.72, s32[1]{0:T(128)} %bitcast.1.g, f32[1024,128]{1,0:T(8,128)} %bitcast.69, f32[1024,128]{1,0:T(8,128)} %bitcast.70, f32[1024,128]{1,0:T(8,128)} %bitcast.71), custom_call_target="tpu_custom_call" | custom-call | flops 10000000 | bytes 4000000 | tf_op jit(solution)/shard_map/windows/pallas_call | solution.py:233
  47.3 11.5 %chip_product.3 = (f32[256,2048]{1,0:T(8,128)}, bf16[256,2048]{1,0:T(8,128)(2,1)}, bf16[256,2048]{1,0:T(8,128)(2,1)}, bf16[256,2048]{1,0:T(8,128)(2,1)}) custom-call(s32[1]{0:T(128)} %bitcast.2.t, bf16[1536,1024]{1,0:T(8,128)(2,1)} %get-tuple-element.57.c, bf16[1536,4096]{1,0:T(8,128)(2,1)} %g.7, bf16[1024,2048]{1,0:T(8,128)(2,1)} %collective-permute-done.1.r), custom_call_target="tpu_custom_call" | custom-call | flops 402653184 | bytes 655360 | tf_op jit(solution)/shard_map/chip_product/pallas_call | solution.py:188
  58.7 2.0 %collective-permute-start.2 = (bf16[3,512,128]{2,1,0:T(8,128)(2,1)}, bf16[3,512,128]{2,1,0:T(8,128)(2,1)S(1)}, u32[]{:S(2)}, u32[]{:S(2)}) collective-permute-start(bf16[3,512,128]{2,1,0:T(8,128)(2,1)} %get-tuple-element.62), channel_id=1, source_target_pairs={{0,32},{1,33},{2,34},{3,35},{4,36},{5,37},{6,38},{7,39},{8,40},{9,... | collective-permute-start | bytes 1179656 | tf_op jit(solution)/shard_map/ppermute | solution.py:268
  60.7 2.2 %collective-permute-start.3 = (bf16[3,512,128]{2,1,0:T(8,128)(2,1)S(1)}, bf16[3,512,128]{2,1,0:T(8,128)(2,1)S(1)}, u32[]{:S(2)}, u32[]{:S(2)}) collective-permute-start(bf16[3,512,128]{2,1,0:T(8,128)(2,1)S(1)} %copy-done.6), channel_id=1, source_target_pairs={{0,96},{1,97},{2,98},{3,99},{4,100},{5,101},{6,102},{7,103},{8,104... | collective-permute-start | bytes 1179656 | tf_op jit(solution)/shard_map/ppermute | solution.py:268
  62.9 3.0 %collective-permute-start.7 = (bf16[256,2048]{1,0:T(8,128)(2,1)}, bf16[256,2048]{1,0:T(8,128)(2,1)}, u32[]{:S(2)}, u32[]{:S(2)}) collective-permute-start(bf16[256,2048]{1,0:T(8,128)(2,1)} %get-tuple-element.76), channel_id=1, source_target_pairs={{0,6},{1,25},{2,0},{3,27},{4,2},{5,29},{6,4},{7,31},{8,14},{9,1},{... | collective-permute-start | bytes 3145736 | tf_op jit(solution)/shard_map/ppermute | solution.py:267
  67.6 4.7 %collective-permute-done.2 = bf16[3,512,128]{2,1,0:T(8,128)(2,1)S(1)} collective-permute-done((bf16[3,512,128]{2,1,0:T(8,128)(2,1)}, bf16[3,512,128]{2,1,0:T(8,128)(2,1)S(1)}, u32[]{:S(2)}, u32[]{:S(2)}) %collective-permute-start.2) | collective-permute-done | bytes 393248 | tf_op jit(solution)/shard_map/ppermute | solution.py:268
  72.4 1.6 %collective-permute-start.4 = (bf16[3,512,128]{2,1,0:T(8,128)(2,1)}, bf16[3,512,128]{2,1,0:T(8,128)(2,1)}, u32[]{:S(2)}, u32[]{:S(2)}) collective-permute-start(bf16[3,512,128]{2,1,0:T(8,128)(2,1)} %get-tuple-element.70), channel_id=1, source_target_pairs={{0,64},{1,65},{2,66},{3,67},{4,68},{5,69},{6,70},{7,71},{8,72},{9,... | collective-permute-start | bytes 1179656 | tf_op jit(solution)/shard_map/ppermute | solution.py:268
  74.7 3.5 %fusion = bf16[256,2048]{1,0:T(8,128)(2,1)} fusion(f32[256,2048]{1,0:T(8,128)S(1)} %copy-done.1, bf16[4,256,2048]{2,1,0:T(8,128)(2,1)} %all-to-all-done, s32[]{:T(128)S(6)} %select_n.82, s32[]{:T(128)S(6)} %select_n.80, s32[]{:T(128)S(6)} %select_n.78), kind=kLoop, calls=%fused_computation.1 | loop fusion | flops 3670016 | bytes 6291468 | tf_op jit(solution)/shard_map/convert_element_type | solution.py:272
  78.2 6.6 %collective-permute-done.4 = bf16[3,512,128]{2,1,0:T(8,128)(2,1)} collective-permute-done((bf16[3,512,128]{2,1,0:T(8,128)(2,1)}, bf16[3,512,128]{2,1,0:T(8,128)(2,1)}, u32[]{:S(2)}, u32[]{:S(2)}) %collective-permute-start.4) | collective-permute-done | bytes 393248 | tf_op jit(solution)/shard_map/ppermute | solution.py:268
  84.8 5.4 %all-to-all-start.1 = ((bf16[16,16,2048]{2,1,0:T(8,128)(2,1)}), bf16[16,16,2048]{2,1,0:T(8,128)(2,1)S(1)}, u32[]{:S(2)}, u32[]{:S(2)}) async-start(bf16[16,16,2048]{2,1,0:T(8,128)(2,1)} %bitcast.11), calls=%async_computation.1 | async-start | bytes 2097152 | tf_op jit(solution)/shard_map/all_to_all | solution.py:276
  90.2 7.0 %collective-permute-done.5 = bf16[256,2048]{1,0:T(8,128)(2,1)} collective-permute-done((bf16[256,2048]{1,0:T(8,128)(2,1)}, bf16[256,2048]{1,0:T(8,128)(2,1)}, u32[]{:S(2)}, u32[]{:S(2)}) %collective-permute-start.5) | collective-permute-done | bytes 1048608 | tf_op jit(solution)/shard_map/ppermute | solution.py:267
  97.3 3.5 %add_convert_fusion = bf16[256,2048]{1,0:T(8,128)(2,1)} fusion(bf16[256,2048]{1,0:T(8,128)(2,1)} %collective-permute-done.7, bf16[256,2048]{1,0:T(8,128)(2,1)} %collective-permute-done.6, f32[256,2048]{1,0:T(8,128)S(1)} %copy-done, bf16[256,2048]{1,0:T(8,128)(2,1)} %collective-permute-done.5), kind=kLoop, calls=%fused_computation.6 | loop fusion | flops 3670016 | bytes 6291456 | tf_op jit(solution)/shard_map/convert_element_type | solution.py:272
  100.8 4.1 %all-to-all-done.1 = bf16[16,16,2048]{2,1,0:T(8,128)(2,1)S(1)} async-done(((bf16[16,16,2048]{2,1,0:T(8,128)(2,1)}), bf16[16,16,2048]{2,1,0:T(8,128)(2,1)S(1)}, u32[]{:S(2)}, u32[]{:S(2)}) %all-to-all-start.1) | async-done | bytes 1048608 | tf_op jit(solution)/shard_map/all_to_all | solution.py:276
  104.9 5.7 %all-to-all-start.2 = ((bf16[16,16,2048]{2,1,0:T(8,128)(2,1)}), bf16[16,16,2048]{2,1,0:T(8,128)(2,1)S(1)}, u32[]{:S(2)}, u32[]{:S(2)}) async-start(bf16[16,16,2048]{2,1,0:T(8,128)(2,1)} %bitcast.15), calls=%async_computation.2 | async-start | bytes 2097152 | tf_op jit(solution)/shard_map/all_to_all | solution.py:276
  110.8 2.1 %convert_add_fusion.3 = f32[3,512,128]{2,1,0:T(8,128)} fusion(bf16[3,512,128]{2,1,0:T(8,128)(2,1)S(1)} %copy-done.5, bf16[3,512,128]{2,1,0:T(8,128)(2,1)} %collective-permute-done.4, bf16[3,512,128]{2,1,0:T(8,128)(2,1)S(1)} %collective-permute-done.2, bf16[3,512,128]{2,1,0:T(8,128)(2,1)S(1)} %copy-done.3), kind=kLoop, calls=%fused_computation.7 | loop fusion | flops 1376256 | bytes 2359296 | tf_op jit(solution)/shard_map/add | solution.py:289
  112.8 1.3 reshape.88
  114.3 9.7 %all-to-all-done.2 = bf16[16,16,2048]{2,1,0:T(8,128)(2,1)S(1)} async-done(((bf16[16,16,2048]{2,1,0:T(8,128)(2,1)}), bf16[16,16,2048]{2,1,0:T(8,128)(2,1)S(1)}, u32[]{:S(2)}, u32[]{:S(2)}) %all-to-all-start.2) | async-done | bytes 1048608 | tf_op jit(solution)/shard_map/all_to_all | solution.py:276
  125.8 2.7 %collective-permute-start.9 = (bf16[16,4096]{1,0:T(8,128)(2,1)S(1)}, bf16[16,4096]{1,0:T(8,128)(2,1)S(1)}, u32[]{:S(2)}, u32[]{:S(2)}) collective-permute-start(bf16[16,4096]{1,0:T(8,128)(2,1)S(1)} %fusion.1), channel_id=1, source_target_pairs={{0,64},{1,65},{2,66},{3,67},{4,68},{5,69},{6,70},{7,71},{8,72},{9,... | collective-permute-start | bytes 393224 | tf_op jit(solution)/shard_map/ppermute | solution.py:294
  128.4 1.2 collective-permute-start.10
  131.5 1.4 %collective-permute-done.9 = bf16[16,4096]{1,0:T(8,128)(2,1)S(1)} collective-permute-done((bf16[16,4096]{1,0:T(8,128)(2,1)S(1)}, bf16[16,4096]{1,0:T(8,128)(2,1)S(1)}, u32[]{:S(2)}, u32[]{:S(2)}) %collective-permute-start.9) | collective-permute-done | bytes 131104 | tf_op jit(solution)/shard_map/ppermute | solution.py:294
  (39 shorter events, 8.5 us)
Async XLA Ops:
  15.3 11.3 %collective-permute-start = (bf16[1024,2048]{1,0:T(8,128)(2,1)}, bf16[1024,2048]{1,0:T(8,128)(2,1)}, u32[]{:S(2)}, u32[]{:S(2)}) collective-permute-start(bf16[1024,2048]{1,0:T(8,128)(2,1)} %get-tuple-element.42), channel_id=1, source_target_pairs={{0,1},{1,0},{2,3},{3,2},{4,5},{5,4},{6,7},{7,6},{8,9},{9,8},{10,11... | collective-permute-start | bytes 12582920 | tf_op jit(solution)/shard_map/ppermute | solution.py:255
  26.2 21.1 %collective-permute-start.1 = (bf16[1024,2048]{1,0:T(8,128)(2,1)}, bf16[1024,2048]{1,0:T(8,128)(2,1)}, u32[]{:S(2)}, u32[]{:S(2)}) collective-permute-start(bf16[1024,2048]{1,0:T(8,128)(2,1)} %other_product.1), channel_id=1, source_target_pairs={{0,1},{1,0},{2,3},{3,2},{4,5},{5,4},{6,7},{7,6},{8,9},{9,8},{10,11... | collective-permute-start | bytes 12582920 | tf_op jit(solution)/shard_map/ppermute | solution.py:257
  38.1 35.9 %all-to-all-start = ((bf16[4,256,2048]{2,1,0:T(8,128)(2,1)}), bf16[4,256,2048]{2,1,0:T(8,128)(2,1)}, u32[]{:S(2)}, u32[]{:S(2)}) async-start(bf16[4,256,2048]{2,1,0:T(8,128)(2,1)} %get-tuple-element.64), calls=%async_computation | async-start | bytes 8388608 | tf_op jit(solution)/shard_map/all_to_all | solution.py:262
  47.3 13.5 %copy-start.6 = (bf16[3,512,128]{2,1,0:T(8,128)(2,1)S(1)}, bf16[3,512,128]{2,1,0:T(8,128)(2,1)}, u32[]{:S(2)}) copy-start(bf16[3,512,128]{2,1,0:T(8,128)(2,1)} %get-tuple-element.63) | copy-start | bytes 1179652
  47.3 27.5 %copy-start.1 = (f32[256,2048]{1,0:T(8,128)S(1)}, f32[256,2048]{1,0:T(8,128)}, u32[]{:S(2)}) copy-start(f32[256,2048]{1,0:T(8,128)} %get-tuple-element.67) | copy-start | bytes 6291460
  58.7 13.6 %collective-permute-start.2 = (bf16[3,512,128]{2,1,0:T(8,128)(2,1)}, bf16[3,512,128]{2,1,0:T(8,128)(2,1)S(1)}, u32[]{:S(2)}, u32[]{:S(2)}) collective-permute-start(bf16[3,512,128]{2,1,0:T(8,128)(2,1)} %get-tuple-element.62), channel_id=1, source_target_pairs={{0,32},{1,33},{2,34},{3,35},{4,36},{5,37},{6,38},{7,39},{8,40},{9,... | collective-permute-start | bytes 1179656 | tf_op jit(solution)/shard_map/ppermute | solution.py:268
  60.7 13.2 %collective-permute-start.3 = (bf16[3,512,128]{2,1,0:T(8,128)(2,1)S(1)}, bf16[3,512,128]{2,1,0:T(8,128)(2,1)S(1)}, u32[]{:S(2)}, u32[]{:S(2)}) collective-permute-start(bf16[3,512,128]{2,1,0:T(8,128)(2,1)S(1)} %copy-done.6), channel_id=1, source_target_pairs={{0,96},{1,97},{2,98},{3,99},{4,100},{5,101},{6,102},{7,103},{8,104... | collective-permute-start | bytes 1179656 | tf_op jit(solution)/shard_map/ppermute | solution.py:268
  62.9 27.3 %collective-permute-start.7 = (bf16[256,2048]{1,0:T(8,128)(2,1)}, bf16[256,2048]{1,0:T(8,128)(2,1)}, u32[]{:S(2)}, u32[]{:S(2)}) collective-permute-start(bf16[256,2048]{1,0:T(8,128)(2,1)} %get-tuple-element.76), channel_id=1, source_target_pairs={{0,6},{1,25},{2,0},{3,27},{4,2},{5,29},{6,4},{7,31},{8,14},{9,1},{... | collective-permute-start | bytes 3145736 | tf_op jit(solution)/shard_map/ppermute | solution.py:267
  65.9 24.3 %collective-permute-start.6 = (bf16[256,2048]{1,0:T(8,128)(2,1)}, bf16[256,2048]{1,0:T(8,128)(2,1)}, u32[]{:S(2)}, u32[]{:S(2)}) collective-permute-start(bf16[256,2048]{1,0:T(8,128)(2,1)} %get-tuple-element.75), channel_id=1, source_target_pairs={{0,4},{1,17},{2,6},{3,19},{4,0},{5,21},{6,2},{7,23},{8,12},{9,25},... | collective-permute-start | bytes 3145736 | tf_op jit(solution)/shard_map/ppermute | solution.py:267
  66.8 30.5 %collective-permute-start.5 = (bf16[256,2048]{1,0:T(8,128)(2,1)}, bf16[256,2048]{1,0:T(8,128)(2,1)}, u32[]{:S(2)}, u32[]{:S(2)}) collective-permute-start(bf16[256,2048]{1,0:T(8,128)(2,1)} %get-tuple-element.74), channel_id=1, source_target_pairs={{0,2},{1,9},{2,4},{3,11},{4,6},{5,13},{6,0},{7,15},{8,10},{9,17},{... | collective-permute-start | bytes 3145736 | tf_op jit(solution)/shard_map/ppermute | solution.py:267
  72.4 12.5 %collective-permute-start.4 = (bf16[3,512,128]{2,1,0:T(8,128)(2,1)}, bf16[3,512,128]{2,1,0:T(8,128)(2,1)}, u32[]{:S(2)}, u32[]{:S(2)}) collective-permute-start(bf16[3,512,128]{2,1,0:T(8,128)(2,1)} %get-tuple-element.70), channel_id=1, source_target_pairs={{0,64},{1,65},{2,66},{3,67},{4,68},{5,69},{6,70},{7,71},{8,72},{9,... | collective-permute-start | bytes 1179656 | tf_op jit(solution)/shard_map/ppermute | solution.py:268
  74.0 0.8 copy-start.4
  78.2 19.1 %copy-start = (f32[256,2048]{1,0:T(8,128)S(1)}, f32[256,2048]{1,0:T(8,128)}, u32[]{:S(2)}) copy-start(f32[256,2048]{1,0:T(8,128)} %get-tuple-element.73) | copy-start | bytes 6291460
  84.8 20.1 %all-to-all-start.1 = ((bf16[16,16,2048]{2,1,0:T(8,128)(2,1)}), bf16[16,16,2048]{2,1,0:T(8,128)(2,1)S(1)}, u32[]{:S(2)}, u32[]{:S(2)}) async-start(bf16[16,16,2048]{2,1,0:T(8,128)(2,1)} %bitcast.11), calls=%async_computation.1 | async-start | bytes 2097152 | tf_op jit(solution)/shard_map/all_to_all | solution.py:276
  100.8 10.0 %copy-start.3 = (bf16[3,512,128]{2,1,0:T(8,128)(2,1)S(1)}, bf16[3,512,128]{2,1,0:T(8,128)(2,1)}, u32[]{:S(2)}) copy-start(bf16[3,512,128]{2,1,0:T(8,128)(2,1)} %get-tuple-element.56) | copy-start | bytes 1179652
  100.8 10.0 %copy-start.5 = (bf16[3,512,128]{2,1,0:T(8,128)(2,1)S(1)}, bf16[3,512,128]{2,1,0:T(8,128)(2,1)}, u32[]{:S(2)}) copy-start(bf16[3,512,128]{2,1,0:T(8,128)(2,1)} %copy-done.4) | copy-start | bytes 1179652
  104.9 19.0 %all-to-all-start.2 = ((bf16[16,16,2048]{2,1,0:T(8,128)(2,1)}), bf16[16,16,2048]{2,1,0:T(8,128)(2,1)S(1)}, u32[]{:S(2)}, u32[]{:S(2)}) async-start(bf16[16,16,2048]{2,1,0:T(8,128)(2,1)} %bitcast.15), calls=%async_computation.2 | async-start | bytes 2097152 | tf_op jit(solution)/shard_map/all_to_all | solution.py:276
  125.2 6.3 %collective-permute-start.8 = (bf16[16,4096]{1,0:T(8,128)(2,1)S(1)}, bf16[16,4096]{1,0:T(8,128)(2,1)S(1)}, u32[]{:S(2)}, u32[]{:S(2)}) collective-permute-start(bf16[16,4096]{1,0:T(8,128)(2,1)S(1)} %fusion.1), channel_id=1, source_target_pairs={{0,32},{1,33},{2,34},{3,35},{4,36},{5,37},{6,38},{7,39},{8,40},{9,... | collective-permute-start | bytes 393224 | tf_op jit(solution)/shard_map/ppermute | solution.py:294
  125.8 7.1 %collective-permute-start.9 = (bf16[16,4096]{1,0:T(8,128)(2,1)S(1)}, bf16[16,4096]{1,0:T(8,128)(2,1)S(1)}, u32[]{:S(2)}, u32[]{:S(2)}) collective-permute-start(bf16[16,4096]{1,0:T(8,128)(2,1)S(1)} %fusion.1), channel_id=1, source_target_pairs={{0,64},{1,65},{2,66},{3,67},{4,68},{5,69},{6,70},{7,71},{8,72},{9,... | collective-permute-start | bytes 393224 | tf_op jit(solution)/shard_map/ppermute | solution.py:294
  128.4 5.3 %collective-permute-start.10 = (bf16[16,4096]{1,0:T(8,128)(2,1)S(1)}, bf16[16,4096]{1,0:T(8,128)(2,1)S(1)}, u32[]{:S(2)}, u32[]{:S(2)}) collective-permute-start(bf16[16,4096]{1,0:T(8,128)(2,1)S(1)} %fusion.1), channel_id=1, source_target_pairs={{0,96},{1,97},{2,98},{3,99},{4,100},{5,101},{6,102},{7,103},{8,104... | collective-permute-start | bytes 393224 | tf_op jit(solution)/shard_map/ppermute | solution.py:294
  133.7 0.8 copy-start.2
